TPU v7x, 1024 devices: a whole 8x8x8 slice. The times are simulated.
1024 devices in a mesh: gx: 16 (over x, y_lo), gy: 64 (over z, y_hi, core).
Axes of the slice: x: 8, y: 8 (y_hi: 4, y_lo: 2; y = y_hi * 2 + y_lo), z: 8, core: 2. Of those that a mesh axis runs over, the one named last changes fastest.
Arguments:
- velocity: float32 [3, 128, 512, 128], P(None, 'gx', 'gy'), may hold values from -6 to 6
- stress: float32 [6, 128, 512, 128], P(None, 'gx', 'gy'), may hold values from -6 to 6
- memory: float32 [6, 128, 512, 128], P(None, 'gx', 'gy'), may hold values from -4 to 4
- material: float32 [3, 128, 512, 128], P(None, 'gx', 'gy'), may hold values from 0.5 to 1.5
- anelastic: float32 [2, 128, 512, 128], P(None, 'gx', 'gy'), may hold values from 0.3 to 0.9
- zone_ids: int32 [128, 512, 128], P('gx', 'gy'), may hold values from 0 to 7
- absorb_mask: int32 [128, 512, 128], P('gx', 'gy'), may hold values 0 or 1
- source_cells: int32 [16, 64, 128], P('gx', 'gy'), may hold values from 0 to 8191
- source_moment: float32 [16, 64, 6, 128], P('gx', 'gy'), may hold values from -6 to 6
- cohesion_table: float32 [8], replicated, may hold values from 0.6 to 1.6
- friction_table: float32 [8], replicated, may hold values from 0.1 to 0.7
Outputs:
- velocity_out: float32 [3, 128, 512, 128], P(None, 'gx', 'gy')
- stress_out: float32 [6, 128, 512, 128], P(None, 'gx', 'gy')
- memory_out: float32 [6, 128, 512, 128], P(None, 'gx', 'gy')
Inputs may be any that keep to these rules, and one draw needn't show every extreme that they name: `source_cells`: p encodes the local cell (p // 1024, (p // 128) % 8, p % 128) of the device's block; several sources may share a cell.
All inputs are finite; a program needn't handle non-finite values. No bound on the sum of `absorb_mask` on one device may be relied on, other than what follows from the above.
Results may differ from a plain program's by a relative error of at most 0.00002.
Values sent between devices are 32-bit elements; how exact they have to be, the bound alone decides.
A program may use at most 32 MiB of HBM per device.

v0:
```python
import jax
import jax.numpy as jnp
from jax import lax
from jax.sharding import PartitionSpec as P

STEPS = 2
ZONES = 8


coef_near = 9.0 / 8.0
coef_far = -1.0 / 24.0
time_ratio = 0.12
sponge_factor = 0.92


def with_halo(cells, sides, width):
    for axis, dim in sides:
        count = lax.axis_size(axis)
        ends = count - 1
        head = lax.slice_in_dim(cells, 0, width, axis=dim)
        tail = lax.slice_in_dim(cells, cells.shape[dim] - width, cells.shape[dim], axis=dim)
        cells = jnp.concatenate(
            [
                lax.ppermute(tail, axis, [(i, (i + 1) % count) for i in range(ends)]),
                cells,
                lax.ppermute(head, axis, [((i + 1) % count, i) for i in range(ends)]),
            ],
            axis=dim,
        )
    return cells


def shifted(field, margin, keep_cycle, shift_x, shift_y, shift_z):
    out_x = field.shape[-3] - 2 * margin + 2 * keep_cycle
    out_y = field.shape[-2] - 2 * margin + 2 * keep_cycle
    out_z = field.shape[-1] - 4
    start_x = margin + shift_x - keep_cycle
    start_y = margin + shift_y - keep_cycle
    start_z = 2 + shift_z
    return field[
        ..., start_x : start_x + out_x, start_y : start_y + out_y, start_z : start_z + out_z
    ]


def offset_view(field, margin, keep_cycle, axis, amount):
    shifts = [0, 0, 0]
    shifts[axis] = amount
    return shifted(field, margin, keep_cycle, shifts[0], shifts[1], shifts[2])


def forward(field, margin, keep_cycle, axis):
    return coef_near * (
        offset_view(field, margin, keep_cycle, axis, 1)
        - offset_view(field, margin, keep_cycle, axis, 0)
    ) + coef_far * (
        offset_view(field, margin, keep_cycle, axis, 2)
        - offset_view(field, margin, keep_cycle, axis, -1)
    )


def backward(field, margin, keep_cycle, axis):
    return coef_near * (
        offset_view(field, margin, keep_cycle, axis, 0)
        - offset_view(field, margin, keep_cycle, axis, -1)
    ) + coef_far * (
        offset_view(field, margin, keep_cycle, axis, 1)
        - offset_view(field, margin, keep_cycle, axis, -2)
    )


def pad_depth(field):
    return jnp.pad(field, [(0, 0)] * (field.ndim - 1) + [(2, 2)])


def velocity_step(stress_pad, margin, keep_cycle, velocity, buoyancy, damping):
    rate_x = (
        forward(stress_pad[0], margin, keep_cycle, 0)
        + backward(stress_pad[3], margin, keep_cycle, 1)
        + backward(stress_pad[4], margin, keep_cycle, 2)
    )
    rate_y = (
        backward(stress_pad[3], margin, keep_cycle, 0)
        + forward(stress_pad[1], margin, keep_cycle, 1)
        + backward(stress_pad[5], margin, keep_cycle, 2)
    )
    rate_z = (
        backward(stress_pad[4], margin, keep_cycle, 0)
        + backward(stress_pad[5], margin, keep_cycle, 1)
        + forward(stress_pad[2], margin, keep_cycle, 2)
    )
    rates = jnp.stack([rate_x, rate_y, rate_z], axis=0)
    return (velocity + time_ratio * buoyancy * rates) * damping


def stress_step(velocity_pad, stress, memory, material, anelastic):
    strain_xx = backward(velocity_pad[0], 2, 0, 0)
    strain_yy = backward(velocity_pad[1], 2, 0, 1)
    strain_zz = backward(velocity_pad[2], 2, 0, 2)
    strain_xy = forward(velocity_pad[0], 2, 0, 1) + forward(velocity_pad[1], 2, 0, 0)
    strain_xz = forward(velocity_pad[0], 2, 0, 2) + forward(velocity_pad[2], 2, 0, 0)
    strain_yz = forward(velocity_pad[1], 2, 0, 2) + forward(velocity_pad[2], 2, 0, 1)
    lame = material[0]
    modulus = material[1]
    volume = strain_xx + strain_yy + strain_zz
    increment = time_ratio * jnp.stack(
        [
            lame * volume + 2.0 * modulus * strain_xx,
            lame * volume + 2.0 * modulus * strain_yy,
            lame * volume + 2.0 * modulus * strain_zz,
            modulus * strain_xy,
            modulus * strain_xz,
            modulus * strain_yz,
        ],
        axis=0,
    )
    memory_new = anelastic[0] * memory + anelastic[1] * increment
    trial = stress + increment - 0.5 * (memory + memory_new)
    return (trial, memory_new)


def zone_values(zone_ids, cohesion_table, friction_table):
    cohesion = jnp.zeros(zone_ids.shape, jnp.float32)
    friction = jnp.zeros(zone_ids.shape, jnp.float32)
    for zone in range(ZONES):
        inside = zone_ids == zone
        cohesion = cohesion + jnp.where(inside, cohesion_table[zone], 0.0)
        friction = friction + jnp.where(inside, friction_table[zone], 0.0)
    return (cohesion, friction)


def add_sources(trial, flat_index, amplitude):
    shape = trial.shape
    flat = trial.reshape(6, -1)
    flat = flat.at[:, flat_index].add(time_ratio * amplitude)
    return flat.reshape(shape)


def yield_limit(trial, cohesion, friction):
    mean_stress = (trial[0] + trial[1] + trial[2]) / 3.0
    return jnp.maximum(cohesion - friction * mean_stress, 0.25 * cohesion)


def below(field):
    return jnp.pad(field, ((0, 0), (0, 0), (1, 0)))[..., :-1]


def above(field):
    return jnp.pad(field, ((0, 0), (0, 0), (0, 1)))[..., 1:]


def plastic_step(extended, trial, upper_x, upper_y):
    size_x = trial.shape[1]
    size_y = trial.shape[2]
    centre = extended[:, 1:, 1:, :]
    mean_stress = (centre[0] + centre[1] + centre[2]) / 3.0
    dev_xx = centre[0] - mean_stress
    dev_yy = centre[1] - mean_stress
    dev_zz = centre[2] - mean_stress
    shear_xy = extended[3]
    centre_xy = 0.25 * (
        shear_xy[:-1, :-1] + shear_xy[:-1, 1:] + shear_xy[1:, :-1] + shear_xy[1:, 1:]
    )
    lower_xz = extended[4][:-1, 1:]
    upper_xz = extended[4][1:, 1:]
    centre_xz = 0.25 * (lower_xz + below(lower_xz) + upper_xz + below(upper_xz))
    lower_yz = extended[5][1:, :-1]
    upper_yz = extended[5][1:, 1:]
    centre_yz = 0.25 * (lower_yz + below(lower_yz) + upper_yz + below(upper_yz))
    tau = jnp.sqrt(
        0.5 * (dev_xx * dev_xx + dev_yy * dev_yy + dev_zz * dev_zz)
        + centre_xy * centre_xy
        + centre_xz * centre_xz
        + centre_yz * centre_yz
    )
    ratio = jnp.minimum(1.0, centre[6] / jnp.maximum(tau, 0.5))
    valid_x = jnp.where(jnp.arange(size_x + 1) < size_x, 1.0, upper_x)
    valid_y = jnp.where(jnp.arange(size_y + 1) < size_y, 1.0, upper_y)
    deficit = (1.0 - ratio) * valid_x[:, None, None] * valid_y[None, :, None]
    factor_xy = 1.0 - 0.25 * (
        deficit[:-1, :-1] + deficit[1:, :-1] + deficit[:-1, 1:] + deficit[1:, 1:]
    )
    first_xz = deficit[:-1, :-1]
    second_xz = deficit[1:, :-1]
    factor_xz = 1.0 - 0.25 * (first_xz + above(first_xz) + second_xz + above(second_xz))
    first_yz = deficit[:-1, :-1]
    second_yz = deficit[:-1, 1:]
    factor_yz = 1.0 - 0.25 * (first_yz + above(first_yz) + second_yz + above(second_yz))
    inner_mean = mean_stress[:-1, :-1]
    inner_ratio = ratio[:-1, :-1]
    return jnp.stack(
        [
            inner_mean + inner_ratio * dev_xx[:-1, :-1],
            inner_mean + inner_ratio * dev_yy[:-1, :-1],
            inner_mean + inner_ratio * dev_zz[:-1, :-1],
            factor_xy * trial[3],
            factor_xz * trial[4],
            factor_yz * trial[5],
        ],
        axis=0,
    )


def shards(
    velocity,
    stress,
    memory,
    material,
    anelastic,
    zone_ids,
    absorb_mask,
    source_cells,
    source_moment,
    cohesion_table,
    friction_table,
):
    damping = jnp.where(absorb_mask == 1, sponge_factor, 1.0).astype(jnp.float32)
    buoyancy = material[2]
    cohesion, friction = zone_values(zone_ids, cohesion_table, friction_table)
    flat_index = source_cells.reshape(-1)
    amplitude = source_moment.reshape(6, -1)
    upper_x = (lax.axis_index("gx") < lax.axis_size("gx") - 1).astype(jnp.float32)
    upper_y = (lax.axis_index("gy") < lax.axis_size("gy") - 1).astype(jnp.float32)
    for time_step in range(STEPS):
        stress_pad = pad_depth(with_halo(stress, (("gx", 1), ("gy", 2)), 2))
        velocity = velocity_step(stress_pad, 2, 0, velocity, buoyancy, damping)
        velocity_pad = pad_depth(with_halo(velocity, (("gx", 1), ("gy", 2)), 2))
        trial, memory = stress_step(velocity_pad, stress, memory, material, anelastic)
        trial = add_sources(trial, flat_index, amplitude)
        limit = yield_limit(trial, cohesion, friction)
        combined = jnp.concatenate([trial, limit[None]], axis=0)
        extended = with_halo(combined, (("gx", 1), ("gy", 2)), 1)
        stress = plastic_step(extended, trial, upper_x, upper_y)
    return (velocity, stress, memory)


def solution(mesh):
    in_specs = (
        P(None, "gx", "gy", None),
        P(None, "gx", "gy", None),
        P(None, "gx", "gy", None),
        P(None, "gx", "gy", None),
        P(None, "gx", "gy", None),
        P("gx", "gy", None),
        P("gx", "gy", None),
        P("gx", "gy", None),
        P("gx", "gy", None, None),
        P(),
        P(),
    )
    out_specs = (P(None, "gx", "gy", None), P(None, "gx", "gy", None), P(None, "gx", "gy", None))
    return jax.shard_map(shards, mesh=mesh, in_specs=in_specs, out_specs=out_specs, check_vma=False)
```

profile of v0, /device:TPU:534, one launch (start us, length us, event | category | flops | bytes accessed | tf_op | source)
XLA Modules:
  0.0 232.9 jit_solution(992914291177984753)
XLA Ops:
  0.6 0.8 fusion.257
  1.5 4.4 %collective-permute-start = (f32[6,2,8,128]{3,2,1,0:T(8,128)S(1)}, f32[6,2,8,128]{3,2,1,0:T(8,128)S(1)}, u32[]{:S(2)}, u32[]{:S(2)}) collective-permute-start(f32[6,2,8,128]{3,2,1,0:T(8,128)S(1)} %get-tuple-element.87), channel_id=1, source_target_pairs={{0,64},{64,128},{128,192},{192,256},{256,320},{320,384},{384,448},... | collective-permute-start | bytes 147464 | tf_op jit(solution)/shard_map/ppermute | solution.py:24
  5.9 1.9 collective-permute-start.1
  7.8 0.8 compare_select_fusion
  8.5 0.8 multiply_bitcast_fusion.1
  9.3 0.8 slice_bitcast_fusion.18
  10.1 0.7 broadcast_multiply_fusion
  10.8 0.9 constant_dynamic-update-slice_fusion.1
  11.7 2.2 collective-permute-done.1
  14.0 1.9 collective-permute-start.2
  15.9 7.9 %collective-permute-start.3 = (f32[6,12,2,128]{3,2,1,0:T(2,128)S(1)}, f32[6,12,2,128]{3,2,1,0:T(2,128)S(1)}, u32[]{:S(2)}, u32[]{:S(2)}) collective-permute-start(f32[6,12,2,128]{3,2,1,0:T(2,128)S(1)} %get-tuple-element.75), channel_id=1, source_target_pairs={{1,0},{2,1},{3,2},{4,3},{5,4},{6,5},{7,6},{8,7},{9,8},{10,9},{11,1... | collective-permute-start | bytes 221192 | tf_op jit(solution)/shard_map/ppermute | solution.py:26
  23.9 1.9 collective-permute-done.3
  25.8 0.7 select_maximum_fusion.4
  27.1 0.3 copy-done.4
  27.5 4.4 %collective-permute-start.4 = (f32[3,2,8,128]{3,2,1,0:T(8,128)S(1)}, f32[3,2,8,128]{3,2,1,0:T(8,128)S(1)}, u32[]{:S(2)}, u32[]{:S(2)}) collective-permute-start(f32[3,2,8,128]{3,2,1,0:T(8,128)S(1)} %get-tuple-element.94), channel_id=1, source_target_pairs={{0,64},{64,128},{128,192},{192,256},{256,320},{320,384},{384,448},... | collective-permute-start | bytes 73736 | tf_op jit(solution)/shard_map/ppermute | solution.py:24
  32.0 1.9 collective-permute-start.5
  33.9 0.7 fusion.267
  34.6 5.2 %collective-permute-done.5 = f32[3,2,8,128]{3,2,1,0:T(8,128)S(1)} collective-permute-done((f32[3,2,8,128]{3,2,1,0:T(8,128)S(1)}, f32[3,2,8,128]{3,2,1,0:T(8,128)S(1)}, u32[]{:S(2)}, u32[]{:S(2)}) %collective-permute-start.5) | collective-permute-done | bytes 24608 | tf_op jit(solution)/shard_map/ppermute | solution.py:26
  39.8 1.9 collective-permute-start.6
  41.7 7.9 %collective-permute-start.7 = (f32[3,12,2,128]{3,2,1,0:T(2,128)S(1)}, f32[3,12,2,128]{3,2,1,0:T(2,128)S(1)}, u32[]{:S(2)}, u32[]{:S(2)}) collective-permute-start(f32[3,12,2,128]{3,2,1,0:T(2,128)S(1)} %get-tuple-element.91), channel_id=1, source_target_pairs={{1,0},{2,1},{3,2},{4,3},{5,4},{6,5},{7,6},{8,7},{9,8},{10,9},{11,1... | collective-permute-start | bytes 110600 | tf_op jit(solution)/shard_map/ppermute | solution.py:26
  49.6 0.7 fusion.266
  50.4 0.8 collective-permute-done.7
  51.2 0.4 select_maximum_fusion.10
  52.3 0.3 copy-done.1
  52.7 2.7 %copy.20 = f32[6,8,8,128]{0,3,2,1:T(8,128)} copy(f32[6,8,8,128]{3,2,1,0:T(8,128)S(1)} %multiply_subtract_fusion.1) | data formatting | bytes 393216 | tf_op jit(solution)/shard_map/sub | solution.py:117
  55.4 5.3 %scatter_custom_fusion = f32[6,8192]{0,1:T(8,128)} fusion(f32[6,8192]{0,1:T(8,128)} %bitcast.267, s32[128]{0:T(128)S(1)} %fusion.248, f32[1,1,6,128]{2,3,0,1:T(8,128)S(1)} %copy.27), kind=kCustom, calls=%fused_computation.157 | custom fusion | flops 768 | bytes 262144 | tf_op jit(solution)/shard_map/scatter-add | solution.py:134
  60.7 18.9 %slice_reduce_fusion.3 = (f32[8192]{0:T(1024)S(1)}, f32[8192]{0:T(1024)S(1)}, f32[8192]{0:T(1024)S(1)}, f32[8192]{0:T(1024)S(1)}) fusion(f32[6,8192]{0,1:T(8,128)} %scatter_custom_fusion), kind=kLoop, calls=%fused_computation.9 | loop fusion | flops 24576 | bytes 327680 | tf_op jit(solution)/shard_map/slice | solution.py:197
  79.7 2.9 %copy.22 = f32[6,8,8,128]{3,2,1,0:T(8,128)S(1)} copy(f32[6,8,8,128]{0,3,2,1:T(8,128)} %bitcast.268) | data formatting | bytes 393216 | tf_op jit(solution)/shard_map/reshape | solution.py:135
  82.6 9.9 %fusion.247 = (f32[1,8,8,128]{3,2,1,0:T(8,128)S(1)}, pred[8,8,128]{2,1,0:T(8,128)(4,1)S(1)}, pred[8,8,128]{2,1,0:T(8,128)(4,1)S(1)}, pred[8,8,128]{2,1,0:T(8,128...) fusion(f32[8192]{0:T(1024)S(1)} %get-tuple-element.9, ...), kind=kLoop, calls=%fused_computation.479 | loop fusion | flops 344064 | bytes 163904 | tf_op jit(solution)/shard_map/broadcast_in_dim | solution.py:230
  92.5 1.9 collective-permute-start.8
  94.5 3.9 %collective-permute-start.9 = (f32[7,1,8,128]{3,2,1,0:T(8,128)S(1)}, f32[7,1,8,128]{3,2,1,0:T(8,128)S(1)}, u32[]{:S(2)}, u32[]{:S(2)}) collective-permute-start(f32[7,1,8,128]{3,2,1,0:T(8,128)S(1)} %get-tuple-element.83), channel_id=1, source_target_pairs={{64,0},{128,64},{192,128},{256,192},{320,256},{384,320},{448,384},... | collective-permute-start | bytes 86024 | tf_op jit(solution)/shard_map/ppermute | solution.py:26
  98.4 3.9 %collective-permute-done.9 = f32[7,1,8,128]{3,2,1,0:T(8,128)S(1)} collective-permute-done((f32[7,1,8,128]{3,2,1,0:T(8,128)S(1)}, f32[7,1,8,128]{3,2,1,0:T(8,128)S(1)}, u32[]{:S(2)}, u32[]{:S(2)}) %collective-permute-start.9) | collective-permute-done | bytes 28704 | tf_op jit(solution)/shard_map/ppermute | solution.py:26
  102.4 6.7 %collective-permute-start.10 = (f32[7,10,1,128]{3,2,1,0:T(1,128)S(1)}, f32[7,10,1,128]{3,2,1,0:T(1,128)S(1)}, u32[]{:S(2)}, u32[]{:S(2)}) collective-permute-start(f32[7,10,1,128]{3,2,1,0:T(1,128)S(1)} %get-tuple-element.79), channel_id=1, source_target_pairs={{1,0},{2,1},{3,2},{4,3},{5,4},{6,5},{7,6},{8,7},{9,8},{10,9},{11,1... | collective-permute-start | bytes 107528 | tf_op jit(solution)/shard_map/ppermute | solution.py:26
  109.1 1.9 collective-permute-start.11
  111.1 7.5 %collective-permute-done.11 = f32[7,10,1,128]{3,2,1,0:T(1,128)S(1)} collective-permute-done((f32[7,10,1,128]{3,2,1,0:T(1,128)S(1)}, f32[7,10,1,128]{3,2,1,0:T(1,128)S(1)}, u32[]{:S(2)}, u32[]{:S(2)}) %collective-permute-start.11) | collective-permute-done | bytes 35872 | tf_op jit(solution)/shard_map/ppermute | solution.py:24
  118.7 0.2 multiply_multiply_fusion.1
  119.2 2.2 collective-permute-start.12
  121.4 3.6 %collective-permute-start.13 = (f32[6,2,8,128]{3,2,1,0:T(8,128)S(1)}, f32[6,2,8,128]{3,2,1,0:T(8,128)S(1)}, u32[]{:S(2)}, u32[]{:S(2)}) collective-permute-start(f32[6,2,8,128]{3,2,1,0:T(8,128)S(1)} %get-tuple-element.85), channel_id=1, source_target_pairs={{64,0},{128,64},{192,128},{256,192},{320,256},{384,320},{448,384},... | collective-permute-start | bytes 147464 | tf_op jit(solution)/shard_map/ppermute | solution.py:26
  125.1 0.6 collective-permute-done.12
  125.7 3.8 %collective-permute-done.13 = f32[6,2,8,128]{3,2,1,0:T(8,128)S(1)} collective-permute-done((f32[6,2,8,128]{3,2,1,0:T(8,128)S(1)}, f32[6,2,8,128]{3,2,1,0:T(8,128)S(1)}, u32[]{:S(2)}, u32[]{:S(2)}) %collective-permute-start.13) | collective-permute-done | bytes 49184 | tf_op jit(solution)/shard_map/ppermute | solution.py:26
  129.6 1.9 collective-permute-start.14
  131.5 7.9 %collective-permute-start.15 = (f32[6,12,2,128]{3,2,1,0:T(2,128)S(1)}, f32[6,12,2,128]{3,2,1,0:T(2,128)S(1)}, u32[]{:S(2)}, u32[]{:S(2)}) collective-permute-start(f32[6,12,2,128]{3,2,1,0:T(2,128)S(1)} %get-tuple-element.73), channel_id=1, source_target_pairs={{1,0},{2,1},{3,2},{4,3},{5,4},{6,5},{7,6},{8,7},{9,8},{10,9},{11,1... | collective-permute-start | bytes 221192 | tf_op jit(solution)/shard_map/ppermute | solution.py:26
  139.5 1.9 collective-permute-done.15
  141.3 0.7 select_maximum_fusion
  142.7 1.9 collective-permute-start.16
  144.7 3.9 %collective-permute-start.17 = (f32[3,2,8,128]{3,2,1,0:T(8,128)S(1)}, f32[3,2,8,128]{3,2,1,0:T(8,128)S(1)}, u32[]{:S(2)}, u32[]{:S(2)}) collective-permute-start(f32[3,2,8,128]{3,2,1,0:T(8,128)S(1)} %get-tuple-element.93), channel_id=1, source_target_pairs={{64,0},{128,64},{192,128},{256,192},{320,256},{384,320},{448,384},... | collective-permute-start | bytes 73736 | tf_op jit(solution)/shard_map/ppermute | solution.py:26
  148.6 3.9 %collective-permute-done.17 = f32[3,2,8,128]{3,2,1,0:T(8,128)S(1)} collective-permute-done((f32[3,2,8,128]{3,2,1,0:T(8,128)S(1)}, f32[3,2,8,128]{3,2,1,0:T(8,128)S(1)}, u32[]{:S(2)}, u32[]{:S(2)}) %collective-permute-start.17) | collective-permute-done | bytes 24608 | tf_op jit(solution)/shard_map/ppermute | solution.py:26
  152.5 1.9 collective-permute-start.18
  154.4 8.0 %collective-permute-start.19 = (f32[3,12,2,128]{3,2,1,0:T(2,128)S(1)}, f32[3,12,2,128]{3,2,1,0:T(2,128)S(1)}, u32[]{:S(2)}, u32[]{:S(2)}) collective-permute-start(f32[3,12,2,128]{3,2,1,0:T(2,128)S(1)} %get-tuple-element.89), channel_id=1, source_target_pairs={{1,0},{2,1},{3,2},{4,3},{5,4},{6,5},{7,6},{8,7},{9,8},{10,9},{11,1... | collective-permute-start | bytes 110600 | tf_op jit(solution)/shard_map/ppermute | solution.py:26
  162.5 1.4 collective-permute-done.19
  163.9 0.4 select_maximum_fusion.6
  165.0 0.8 multiply_subtract_fusion
  165.8 2.7 %copy.23 = f32[6,8,8,128]{0,3,2,1:T(8,128)} copy(f32[6,8,8,128]{3,2,1,0:T(8,128)S(1)} %get-tuple-element.17) | data formatting | bytes 393216 | tf_op jit(solution)/shard_map/sub | solution.py:117
  168.4 5.3 %scatter_custom_fusion.1 = f32[6,8192]{0,1:T(8,128)} fusion(f32[6,8192]{0,1:T(8,128)} %bitcast.265, s32[128]{0:T(128)S(1)} %fusion.248, f32[1,1,6,128]{2,3,0,1:T(8,128)S(1)} %copy.27), kind=kCustom, calls=%fused_computation.155 | custom fusion | flops 768 | bytes 262144 | tf_op jit(solution)/shard_map/scatter-add | solution.py:134
  173.7 18.9 %slice_reduce_fusion = (f32[8192]{0:T(1024)S(1)}, f32[8192]{0:T(1024)S(1)}, f32[8192]{0:T(1024)S(1)}, f32[8192]{0:T(1024)S(1)}) fusion(f32[6,8192]{0,1:T(8,128)} %scatter_custom_fusion.1), kind=kLoop, calls=%fused_computation.2 | loop fusion | flops 24576 | bytes 327680 | tf_op jit(solution)/shard_map/slice | solution.py:197
  192.7 2.9 %copy.25 = f32[6,8,8,128]{3,2,1,0:T(8,128)S(1)} copy(f32[6,8,8,128]{0,3,2,1:T(8,128)} %bitcast.266) | data formatting | bytes 393216 | tf_op jit(solution)/shard_map/reshape | solution.py:135
  195.6 9.9 %fusion.244 = f32[1,8,8,128]{3,2,1,0:T(8,128)S(1)} fusion(f32[8192]{0:T(1024)S(1)} %get-tuple-element.5, pred[8,8,128]{2,1,0:T(8,128)(4,1)S(1)} %get-tuple-element.37, f32[]{:T(128)} %bitcast.35, pred[8,8,128]{2,1,0:T(8,128)(4,1)S(1)} %get-tuple-element.36, f32[]{:T(128)} %bitcast.34, pred[8,8,128]{2,1,0:T(8,128)(4,1)S(1)} %get-tuple-element.35, ...), kind=kLoop, calls=%fused_computation.475 | loop fusion | flops 278528 | bytes 131136 | tf_op jit(solution)/shard_map/broadcast_in_dim | solution.py:230
  205.5 1.9 collective-permute-start.20
  207.4 3.9 %collective-permute-start.21 = (f32[7,1,8,128]{3,2,1,0:T(8,128)S(1)}, f32[7,1,8,128]{3,2,1,0:T(8,128)S(1)}, u32[]{:S(2)}, u32[]{:S(2)}) collective-permute-start(f32[7,1,8,128]{3,2,1,0:T(8,128)S(1)} %get-tuple-element.81), channel_id=1, source_target_pairs={{64,0},{128,64},{192,128},{256,192},{320,256},{384,320},{448,384},... | collective-permute-start | bytes 86024 | tf_op jit(solution)/shard_map/ppermute | solution.py:26
  211.4 3.9 %collective-permute-done.21 = f32[7,1,8,128]{3,2,1,0:T(8,128)S(1)} collective-permute-done((f32[7,1,8,128]{3,2,1,0:T(8,128)S(1)}, f32[7,1,8,128]{3,2,1,0:T(8,128)S(1)}, u32[]{:S(2)}, u32[]{:S(2)}) %collective-permute-start.21) | collective-permute-done | bytes 28704 | tf_op jit(solution)/shard_map/ppermute | solution.py:26
  215.4 6.7 %collective-permute-start.22 = (f32[7,10,1,128]{3,2,1,0:T(1,128)S(1)}, f32[7,10,1,128]{3,2,1,0:T(1,128)S(1)}, u32[]{:S(2)}, u32[]{:S(2)}) collective-permute-start(f32[7,10,1,128]{3,2,1,0:T(1,128)S(1)} %get-tuple-element.77), channel_id=1, source_target_pairs={{1,0},{2,1},{3,2},{4,3},{5,4},{6,5},{7,6},{8,7},{9,8},{10,9},{11,1... | collective-permute-start | bytes 107528 | tf_op jit(solution)/shard_map/ppermute | solution.py:26
  222.1 1.9 collective-permute-start.23
  224.0 7.5 %collective-permute-done.23 = f32[7,10,1,128]{3,2,1,0:T(1,128)S(1)} collective-permute-done((f32[7,10,1,128]{3,2,1,0:T(1,128)S(1)}, f32[7,10,1,128]{3,2,1,0:T(1,128)S(1)}, u32[]{:S(2)}, u32[]{:S(2)}) %collective-permute-start.23) | collective-permute-done | bytes 35872 | tf_op jit(solution)/shard_map/ppermute | solution.py:24
  232.2 0.7 copy-done.8
  (91 shorter events, 4.2 us)
Async XLA Ops:
  0.6 23.2 %copy-start.9 = (s32[1,1,128]{2,1,0:T(1,128)S(1)}, s32[1,1,128]{2,1,0:T(1,128)}, u32[]{:S(2)}) copy-start(s32[1,1,128]{2,1,0:T(1,128)} %param.18) | copy-start | bytes 1540
  1.5 9.3 %collective-permute-start = (f32[6,2,8,128]{3,2,1,0:T(8,128)S(1)}, f32[6,2,8,128]{3,2,1,0:T(8,128)S(1)}, u32[]{:S(2)}, u32[]{:S(2)}) collective-permute-start(f32[6,2,8,128]{3,2,1,0:T(8,128)S(1)} %get-tuple-element.87), channel_id=1, source_target_pairs={{0,64},{64,128},{128,192},{192,256},{256,320},{320,384},{384,448},... | collective-permute-start | bytes 147464 | tf_op jit(solution)/shard_map/ppermute | solution.py:24
  5.9 8.1 %collective-permute-start.1 = (f32[6,2,8,128]{3,2,1,0:T(8,128)S(1)}, f32[6,2,8,128]{3,2,1,0:T(8,128)S(1)}, u32[]{:S(2)}, u32[]{:S(2)}) collective-permute-start(f32[6,2,8,128]{3,2,1,0:T(8,128)S(1)} %get-tuple-element.86), channel_id=1, source_target_pairs={{64,0},{128,64},{192,128},{256,192},{320,256},{384,320},{448,384},... | collective-permute-start | bytes 147464 | tf_op jit(solution)/shard_map/ppermute | solution.py:26
  14.0 9.9 %collective-permute-start.2 = (f32[6,12,2,128]{3,2,1,0:T(2,128)S(1)}, f32[6,12,2,128]{3,2,1,0:T(2,128)S(1)}, u32[]{:S(2)}, u32[]{:S(2)}) collective-permute-start(f32[6,12,2,128]{3,2,1,0:T(2,128)S(1)} %get-tuple-element.74), channel_id=1, source_target_pairs={{0,1},{1,2},{2,3},{3,4},{4,5},{5,6},{6,7},{7,8},{8,9},{9,10},{10,1... | collective-permute-start | bytes 221192 | tf_op jit(solution)/shard_map/ppermute | solution.py:24
  15.9 9.8 %collective-permute-start.3 = (f32[6,12,2,128]{3,2,1,0:T(2,128)S(1)}, f32[6,12,2,128]{3,2,1,0:T(2,128)S(1)}, u32[]{:S(2)}, u32[]{:S(2)}) collective-permute-start(f32[6,12,2,128]{3,2,1,0:T(2,128)S(1)} %get-tuple-element.75), channel_id=1, source_target_pairs={{1,0},{2,1},{3,2},{4,3},{5,4},{6,5},{7,6},{8,7},{9,8},{10,9},{11,1... | collective-permute-start | bytes 221192 | tf_op jit(solution)/shard_map/ppermute | solution.py:26
  26.6 0.9 copy-start.4
  26.6 7.3 %copy-start.5 = (f32[8]{0:T(128)S(1)}, f32[8]{0:T(128)}, u32[]{:S(2)}) copy-start(f32[8]{0:T(128)} %param.20) | copy-start | bytes 100
  26.6 23.0 %copy-start.6 = (f32[8]{0:T(128)S(1)}, f32[8]{0:T(128)}, u32[]{:S(2)}) copy-start(f32[8]{0:T(128)} %param.21) | copy-start | bytes 100
  27.5 24.2 %copy-start = (f32[3,8,8,128]{3,2,1,0:T(8,128)S(1)}, f32[3,8,8,128]{3,2,1,0:T(8,128)}, u32[]{:S(2)}) copy-start(f32[3,8,8,128]{3,2,1,0:T(8,128)} %param.14) | copy-start | bytes 294916
  27.5 7.0 %collective-permute-start.4 = (f32[3,2,8,128]{3,2,1,0:T(8,128)S(1)}, f32[3,2,8,128]{3,2,1,0:T(8,128)S(1)}, u32[]{:S(2)}, u32[]{:S(2)}) collective-permute-start(f32[3,2,8,128]{3,2,1,0:T(8,128)S(1)} %get-tuple-element.94), channel_id=1, source_target_pairs={{0,64},{64,128},{128,192},{192,256},{256,320},{320,384},{384,448},... | collective-permute-start | bytes 73736 | tf_op jit(solution)/shard_map/ppermute | solution.py:24
  32.0 7.8 %collective-permute-start.5 = (f32[3,2,8,128]{3,2,1,0:T(8,128)S(1)}, f32[3,2,8,128]{3,2,1,0:T(8,128)S(1)}, u32[]{:S(2)}, u32[]{:S(2)}) collective-permute-start(f32[3,2,8,128]{3,2,1,0:T(8,128)S(1)} %get-tuple-element.95), channel_id=1, source_target_pairs={{64,0},{128,64},{192,128},{256,192},{320,256},{384,320},{448,384},... | collective-permute-start | bytes 73736 | tf_op jit(solution)/shard_map/ppermute | solution.py:26
  39.8 10.6 %collective-permute-start.6 = (f32[3,12,2,128]{3,2,1,0:T(2,128)S(1)}, f32[3,12,2,128]{3,2,1,0:T(2,128)S(1)}, u32[]{:S(2)}, u32[]{:S(2)}) collective-permute-start(f32[3,12,2,128]{3,2,1,0:T(2,128)S(1)} %get-tuple-element.90), channel_id=1, source_target_pairs={{0,1},{1,2},{2,3},{3,4},{4,5},{5,6},{6,7},{7,8},{8,9},{9,10},{10,1... | collective-permute-start | bytes 110600 | tf_op jit(solution)/shard_map/ppermute | solution.py:24
  41.7 9.5 %collective-permute-start.7 = (f32[3,12,2,128]{3,2,1,0:T(2,128)S(1)}, f32[3,12,2,128]{3,2,1,0:T(2,128)S(1)}, u32[]{:S(2)}, u32[]{:S(2)}) collective-permute-start(f32[3,12,2,128]{3,2,1,0:T(2,128)S(1)} %get-tuple-element.91), channel_id=1, source_target_pairs={{1,0},{2,1},{3,2},{4,3},{5,4},{6,5},{7,6},{8,7},{9,8},{10,9},{11,1... | collective-permute-start | bytes 110600 | tf_op jit(solution)/shard_map/ppermute | solution.py:26
  51.6 0.9 copy-start.1
  51.7 1.0 copy-start.3
  79.7 2.9 %copy-start.7 = (s32[8,8,128]{2,1,0:T(8,128)S(1)}, s32[8,8,128]{2,1,0:T(8,128)}, u32[]{:S(2)}) copy-start(s32[8,8,128]{2,1,0:T(8,128)} %param.16) | copy-start | bytes 98308
  92.5 5.9 %collective-permute-start.8 = (f32[7,1,8,128]{3,2,1,0:T(8,128)S(1)}, f32[7,1,8,128]{3,2,1,0:T(8,128)S(1)}, u32[]{:S(2)}, u32[]{:S(2)}) collective-permute-start(f32[7,1,8,128]{3,2,1,0:T(8,128)S(1)} %get-tuple-element.82), channel_id=1, source_target_pairs={{0,64},{64,128},{128,192},{192,256},{256,320},{320,384},{384,448},... | collective-permute-start | bytes 86024 | tf_op jit(solution)/shard_map/ppermute | solution.py:24
  94.5 7.9 %collective-permute-start.9 = (f32[7,1,8,128]{3,2,1,0:T(8,128)S(1)}, f32[7,1,8,128]{3,2,1,0:T(8,128)S(1)}, u32[]{:S(2)}, u32[]{:S(2)}) collective-permute-start(f32[7,1,8,128]{3,2,1,0:T(8,128)S(1)} %get-tuple-element.83), channel_id=1, source_target_pairs={{64,0},{128,64},{192,128},{256,192},{320,256},{384,320},{448,384},... | collective-permute-start | bytes 86024 | tf_op jit(solution)/shard_map/ppermute | solution.py:26
  102.4 8.7 %collective-permute-start.10 = (f32[7,10,1,128]{3,2,1,0:T(1,128)S(1)}, f32[7,10,1,128]{3,2,1,0:T(1,128)S(1)}, u32[]{:S(2)}, u32[]{:S(2)}) collective-permute-start(f32[7,10,1,128]{3,2,1,0:T(1,128)S(1)} %get-tuple-element.79), channel_id=1, source_target_pairs={{1,0},{2,1},{3,2},{4,3},{5,4},{6,5},{7,6},{8,7},{9,8},{10,9},{11,1... | collective-permute-start | bytes 107528 | tf_op jit(solution)/shard_map/ppermute | solution.py:26
  109.1 9.5 %collective-permute-start.11 = (f32[7,10,1,128]{3,2,1,0:T(1,128)S(1)}, f32[7,10,1,128]{3,2,1,0:T(1,128)S(1)}, u32[]{:S(2)}, u32[]{:S(2)}) collective-permute-start(f32[7,10,1,128]{3,2,1,0:T(1,128)S(1)} %get-tuple-element.78), channel_id=1, source_target_pairs={{0,1},{1,2},{2,3},{3,4},{4,5},{5,6},{6,7},{7,8},{8,9},{9,10},{10,1... | collective-permute-start | bytes 107528 | tf_op jit(solution)/shard_map/ppermute | solution.py:24
  119.2 6.5 %collective-permute-start.12 = (f32[6,2,8,128]{3,2,1,0:T(8,128)S(1)}, f32[6,2,8,128]{3,2,1,0:T(8,128)S(1)}, u32[]{:S(2)}, u32[]{:S(2)}) collective-permute-start(f32[6,2,8,128]{3,2,1,0:T(8,128)S(1)} %get-tuple-element.84), channel_id=1, source_target_pairs={{0,64},{64,128},{128,192},{192,256},{256,320},{320,384},{384,448},... | collective-permute-start | bytes 147464 | tf_op jit(solution)/shard_map/ppermute | solution.py:24
  121.4 8.1 %collective-permute-start.13 = (f32[6,2,8,128]{3,2,1,0:T(8,128)S(1)}, f32[6,2,8,128]{3,2,1,0:T(8,128)S(1)}, u32[]{:S(2)}, u32[]{:S(2)}) collective-permute-start(f32[6,2,8,128]{3,2,1,0:T(8,128)S(1)} %get-tuple-element.85), channel_id=1, source_target_pairs={{64,0},{128,64},{192,128},{256,192},{320,256},{384,320},{448,384},... | collective-permute-start | bytes 147464 | tf_op jit(solution)/shard_map/ppermute | solution.py:26
  129.6 9.9 %collective-permute-start.14 = (f32[6,12,2,128]{3,2,1,0:T(2,128)S(1)}, f32[6,12,2,128]{3,2,1,0:T(2,128)S(1)}, u32[]{:S(2)}, u32[]{:S(2)}) collective-permute-start(f32[6,12,2,128]{3,2,1,0:T(2,128)S(1)} %get-tuple-element.72), channel_id=1, source_target_pairs={{0,1},{1,2},{2,3},{3,4},{4,5},{5,6},{6,7},{7,8},{8,9},{9,10},{10,1... | collective-permute-start | bytes 221192 | tf_op jit(solution)/shard_map/ppermute | solution.py:24
  131.5 9.8 %collective-permute-start.15 = (f32[6,12,2,128]{3,2,1,0:T(2,128)S(1)}, f32[6,12,2,128]{3,2,1,0:T(2,128)S(1)}, u32[]{:S(2)}, u32[]{:S(2)}) collective-permute-start(f32[6,12,2,128]{3,2,1,0:T(2,128)S(1)} %get-tuple-element.73), channel_id=1, source_target_pairs={{1,0},{2,1},{3,2},{4,3},{5,4},{6,5},{7,6},{8,7},{9,8},{10,9},{11,1... | collective-permute-start | bytes 221192 | tf_op jit(solution)/shard_map/ppermute | solution.py:26
  142.7 21.8 %copy-start.2 = (f32[3,8,8,128]{3,2,1,0:T(8,128)}, f32[3,8,8,128]{3,2,1,0:T(8,128)S(1)}, u32[]{:S(2)}) copy-start(f32[3,8,8,128]{3,2,1,0:T(8,128)S(1)} %fusion.9) | copy-start | bytes 294916
  142.7 5.9 %collective-permute-start.16 = (f32[3,2,8,128]{3,2,1,0:T(8,128)S(1)}, f32[3,2,8,128]{3,2,1,0:T(8,128)S(1)}, u32[]{:S(2)}, u32[]{:S(2)}) collective-permute-start(f32[3,2,8,128]{3,2,1,0:T(8,128)S(1)} %get-tuple-element.92), channel_id=1, source_target_pairs={{0,64},{64,128},{128,192},{192,256},{256,320},{320,384},{384,448},... | collective-permute-start | bytes 73736 | tf_op jit(solution)/shard_map/ppermute | solution.py:24
  144.7 7.8 %collective-permute-start.17 = (f32[3,2,8,128]{3,2,1,0:T(8,128)S(1)}, f32[3,2,8,128]{3,2,1,0:T(8,128)S(1)}, u32[]{:S(2)}, u32[]{:S(2)}) collective-permute-start(f32[3,2,8,128]{3,2,1,0:T(8,128)S(1)} %get-tuple-element.93), channel_id=1, source_target_pairs={{64,0},{128,64},{192,128},{256,192},{320,256},{384,320},{448,384},... | collective-permute-start | bytes 73736 | tf_op jit(solution)/shard_map/ppermute | solution.py:26
  152.5 10.0 %collective-permute-start.18 = (f32[3,12,2,128]{3,2,1,0:T(2,128)S(1)}, f32[3,12,2,128]{3,2,1,0:T(2,128)S(1)}, u32[]{:S(2)}, u32[]{:S(2)}) collective-permute-start(f32[3,12,2,128]{3,2,1,0:T(2,128)S(1)} %get-tuple-element.88), channel_id=1, source_target_pairs={{0,1},{1,2},{2,3},{3,4},{4,5},{5,6},{6,7},{7,8},{8,9},{9,10},{10,1... | collective-permute-start | bytes 110600 | tf_op jit(solution)/shard_map/ppermute | solution.py:24
  154.4 9.5 %collective-permute-start.19 = (f32[3,12,2,128]{3,2,1,0:T(2,128)S(1)}, f32[3,12,2,128]{3,2,1,0:T(2,128)S(1)}, u32[]{:S(2)}, u32[]{:S(2)}) collective-permute-start(f32[3,12,2,128]{3,2,1,0:T(2,128)S(1)} %get-tuple-element.89), channel_id=1, source_target_pairs={{1,0},{2,1},{3,2},{4,3},{5,4},{6,5},{7,6},{8,7},{9,8},{10,9},{11,1... | collective-permute-start | bytes 110600 | tf_op jit(solution)/shard_map/ppermute | solution.py:26
  205.5 5.9 %collective-permute-start.20 = (f32[7,1,8,128]{3,2,1,0:T(8,128)S(1)}, f32[7,1,8,128]{3,2,1,0:T(8,128)S(1)}, u32[]{:S(2)}, u32[]{:S(2)}) collective-permute-start(f32[7,1,8,128]{3,2,1,0:T(8,128)S(1)} %get-tuple-element.80), channel_id=1, source_target_pairs={{0,64},{64,128},{128,192},{192,256},{256,320},{320,384},{384,448},... | collective-permute-start | bytes 86024 | tf_op jit(solution)/shard_map/ppermute | solution.py:24
  207.4 7.9 %collective-permute-start.21 = (f32[7,1,8,128]{3,2,1,0:T(8,128)S(1)}, f32[7,1,8,128]{3,2,1,0:T(8,128)S(1)}, u32[]{:S(2)}, u32[]{:S(2)}) collective-permute-start(f32[7,1,8,128]{3,2,1,0:T(8,128)S(1)} %get-tuple-element.81), channel_id=1, source_target_pairs={{64,0},{128,64},{192,128},{256,192},{320,256},{384,320},{448,384},... | collective-permute-start | bytes 86024 | tf_op jit(solution)/shard_map/ppermute | solution.py:26
  215.4 8.7 %collective-permute-start.22 = (f32[7,10,1,128]{3,2,1,0:T(1,128)S(1)}, f32[7,10,1,128]{3,2,1,0:T(1,128)S(1)}, u32[]{:S(2)}, u32[]{:S(2)}) collective-permute-start(f32[7,10,1,128]{3,2,1,0:T(1,128)S(1)} %get-tuple-element.77), channel_id=1, source_target_pairs={{1,0},{2,1},{3,2},{4,3},{5,4},{6,5},{7,6},{8,7},{9,8},{10,9},{11,1... | collective-permute-start | bytes 107528 | tf_op jit(solution)/shard_map/ppermute | solution.py:26
  222.1 9.5 %collective-permute-start.23 = (f32[7,10,1,128]{3,2,1,0:T(1,128)S(1)}, f32[7,10,1,128]{3,2,1,0:T(1,128)S(1)}, u32[]{:S(2)}, u32[]{:S(2)}) collective-permute-start(f32[7,10,1,128]{3,2,1,0:T(1,128)S(1)} %get-tuple-element.76), channel_id=1, source_target_pairs={{0,1},{1,2},{2,3},{3,4},{4,5},{5,6},{6,7},{7,8},{8,9},{9,10},{10,1... | collective-permute-start | bytes 107528 | tf_op jit(solution)/shard_map/ppermute | solution.py:24
  232.2 0.7 copy-start.8
where the time goes:
time: 234 us; the launch traced here: 233 us
  starting transfers between devices  92.6 us (40%)
  other arithmetic  77.6 us (33%)
  waiting for transfers between devices  44.8 us (19%)
  local copies, waits for them, and re-layouts  16.3 us (7%)
    ppermute x12, starting transfers between devices, with_halo(): lax.ppermute(head, axis, [((i + 1) % count, i) for i in range(ends)])  64.3 us
    slice x2, other arithmetic, plastic_step(): trial[5]  37.9 us
    ppermute x12, waiting for transfers between devices, with_halo(): lax.ppermute(head, axis, [((i + 1) % count, i) for i in range(ends)])  29 us
    ppermute x12, starting transfers between devices, with_halo(): lax.ppermute(tail, axis, [(i, (i + 1) % count) for i in range(ends)])  28.3 us
    broadcast_in_dim x2, other arithmetic, shards(): combined = jnp.concatenate([trial, limit[None]], axis=0)  19.8 us
    ppermute x12, waiting for transfers between devices, with_halo(): lax.ppermute(tail, axis, [(i, (i + 1) % count) for i in range(ends)])  15.9 us
    scatter-add x2, other arithmetic, add_sources(): flat = flat.at[:, flat_index].add(time_ratio * amplitude)  10.6 us
    reshape x2, local copies, waits for them, and re-layouts, add_sources(): return flat.reshape(shape)  5.77 us
  transfers between devices with their start and end apart: 24, of which 15 were waited for; matrix products, arithmetic and copies ran while one was open for 2% of the time, Pallas kernels for 0%

commit v1 on v0

v1 whole, which is shorter than its diff:
```python
import functools

import jax
import jax.numpy as jnp
from jax import lax
from jax.experimental import pallas as pl
from jax.experimental.pallas import tpu as pltpu
from jax.sharding import PartitionSpec as P

MESH = pl.DeviceIdType.MESH
STEPS = 2
ZONES = 8
NEAR = 9.0 / 8.0
FAR = -1.0 / 24.0
H = 0.12
SPONGE = 0.92
OPEN = 1.0e9

SXX, SXY, SXZ, SYY, SYZ, VX, VY, VZ = range(8)
CXX, CYY, CZZ, CXY, CXZ, CYZ = range(8, 14)
PP, QQ, COH, FRI = range(14, 18)
TXY, UXZ, UYZ, DEF, DEZ = range(18, 23)
FIELDS = 23
SLABS = 14
PITCH = 16

FACES = ((-1, 0), (1, 0), (0, -1), (0, 1))
CORNERS = ((-1, -1), (-1, 1), (1, -1), (1, 1))
SIDES = FACES + CORNERS


def row(x, y):
    return (x + 3) * PITCH + (y + 4)


def xs(field, x):
    return (field, "B", x, 0, 8)


def ys(field, y):
    return (field, "F", 0, y, 8)


def some(field, x, y, n=1):
    return (field, "B", x, y, n)


STRESS_SENT = {
    (1, 0): [xs(SXX, 7), xs(SXY, 6), xs(SXY, 7), xs(SXZ, 6), xs(SXZ, 7)],
    (-1, 0): [xs(SXX, 0), xs(SXX, 1), xs(SXY, 0), xs(SXZ, 0)],
    (0, 1): [ys(SYY, 7), ys(SXY, 6), ys(SXY, 7), ys(SYZ, 6), ys(SYZ, 7)],
    (0, -1): [ys(SYY, 0), ys(SYY, 1), ys(SXY, 0), ys(SYZ, 0)],
}
BASE_SENT = {
    (1, 0): [xs(CXY, 7), xs(CXZ, 7)],
    (-1, 0): [xs(f, 0) for f in (CXX, CYY, CZZ, CXY, CXZ, CYZ)],
    (0, 1): [ys(CXY, 7), ys(CYZ, 7)],
    (0, -1): [ys(f, 0) for f in (CXX, CYY, CZZ, CXY, CXZ, CYZ)],
}
FIXED_SENT = {
    (1, 0): [xs(QQ, 7)],
    (-1, 0): [xs(f, 0) for f in (PP, QQ, COH, FRI)],
    (0, 1): [ys(QQ, 7)],
    (0, -1): [ys(f, 0) for f in (PP, QQ, COH, FRI)],
    (1, 1): [some(QQ, 7, 7)],
    (-1, -1): [some(f, 0, 0) for f in (PP, QQ, COH, FRI)],
    (-1, 1): [some(QQ, 0, 7)],
    (1, -1): [some(QQ, 7, 0)],
}
VELOCITY_SENT = {
    (1, 0): [xs(f, x) for f in (VX, VY, VZ) for x in (6, 7)],
    (-1, 0): [xs(f, x) for f, n in ((VX, 2), (VY, 3), (VZ, 3)) for x in range(n)],
    (0, 1): [ys(f, y) for f in (VX, VY, VZ) for y in (6, 7)],
    (0, -1): [ys(f, y) for f, n in ((VX, 3), (VY, 2), (VZ, 3)) for y in range(n)],
    (1, 1): [some(VX, 7, 6, 2), some(VY, 6, 7), some(VY, 7, 7), some(CXY, 7, 7)],
    (-1, -1): [
        some(VX, 0, 0, 3),
        some(VX, 1, 0),
        some(VY, 0, 0, 2),
        some(VY, 1, 0),
        some(VY, 2, 0),
        some(VZ, 0, 0, 3),
        some(VZ, 1, 0),
        some(VZ, 2, 0),
    ]
    + [some(f, 0, 0) for f in (CXX, CYY, CZZ, CXY, CXZ, CYZ)],
    (-1, 1): [
        some(VX, 0, 6, 2),
        some(VY, 0, 6, 2),
        some(VY, 1, 7),
        some(VY, 2, 7),
        some(VZ, 0, 6, 2),
        some(CXY, 0, 7),
        some(CYZ, 0, 7),
    ],
    (1, -1): [
        some(VX, 7, 0, 3),
        some(VX, 6, 0),
        some(VY, 6, 0),
        some(VY, 7, 0),
        some(VZ, 6, 0),
        some(VZ, 7, 0),
        some(CXY, 7, 0),
        some(CXZ, 7, 0),
    ],
}


def joined(*tables):
    return {d: sum((t.get(d, []) for t in tables), []) for d in SIDES if any(d in t for t in tables)}


def rows_of(items):
    return -(-sum(item[4] for item in items) // 8) * 8


MESSAGES = []
for first in (True, False):
    MESSAGES.append(STRESS_SENT)
    faces_fixed = {d: FIXED_SENT[d] for d in FACES}
    MESSAGES.append(joined(BASE_SENT, faces_fixed) if first else BASE_SENT)
    corners_fixed = {d: FIXED_SENT[d] for d in CORNERS}
    MESSAGES.append(joined(VELOCITY_SENT, corners_fixed) if first else VELOCITY_SENT)

PLACES = {}
used = 0
for kind, table in enumerate(MESSAGES):
    for side, sent in table.items():
        PLACES[kind, side] = (used, rows_of(sent), len(PLACES))
        used += rows_of(sent)
BUFFER_ROWS = used
N_MESSAGES = len(PLACES)


def kernel(
    n_gx,
    n_gy,
    velocity_in,
    stress_in,
    memory_in,
    material_in,
    anelastic_in,
    zone_in,
    absorb_in,
    cells_in,
    moment_in,
    cohesion_table,
    friction_table,
    velocity_out,
    stress_out,
    memory_out,
    ext,
    sent,
    received,
    velocity,
    stress,
    memory,
    material,
    anelastic,
    zone,
    absorb,
    cells,
    moment,
    source,
    weight,
    centre,
    send_sem,
    recv_sem,
    in_sem,
    out_sem,
):
    gx, gy = lax.axis_index("gx"), lax.axis_index("gy")
    there = {}
    for dx, dy in SIDES:
        checks = []
        if dx:
            checks.append(gx > 0 if dx < 0 else gx < n_gx - 1)
        if dy:
            checks.append(gy > 0 if dy < 0 else gy < n_gy - 1)
        there[dx, dy] = checks[0] if len(checks) == 1 else jnp.logical_and(*checks)

    def device(d):
        return (gx + d[0], gy + d[1])

    barrier = pltpu.get_barrier_semaphore()
    for d in SIDES:

        @pl.when(there[d])
        def _():
            pl.semaphore_signal(barrier, 1, device_id=device(d), device_id_type=MESH)

    loads = []
    for k, (src, dst) in enumerate(
        (
            (stress_in, stress),
            (velocity_in, velocity),
            (memory_in, memory),
            (material_in, material),
            (anelastic_in, anelastic),
            (zone_in, zone),
            (absorb_in, absorb),
            (cells_in, cells),
            (moment_in, moment),
        )
    ):
        loads.append(pltpu.make_async_copy(src, dst, in_sem.at[k]))
        loads[-1].start()

    def at(item, d=(0, 0)):
        field, form, x, y, n = item
        start = row(x - 8 * d[0], y - 8 * d[1])
        return ext.at[field, pl.ds(start, n) if form == "B" else pl.ds(start, n, stride=PITCH), :]

    def copy_of(kind, d, sem_side):
        start, n, k = PLACES[kind, d]
        return pltpu.make_async_remote_copy(
            src_ref=sent.at[pl.ds(start, n)],
            dst_ref=received.at[pl.ds(start, n)],
            send_sem=send_sem.at[k],
            recv_sem=recv_sem.at[k],
            device_id=device(sem_side),
            device_id_type=MESH,
        )

    def pack(kind):
        for d, items in MESSAGES[kind].items():
            start = PLACES[kind, d][0]
            for item in items:
                sent[pl.ds(start, item[4]), :] = at(item)[...]
                start += item[4]

    def send(kind):
        for d in MESSAGES[kind]:

            @pl.when(there[d])
            def _():
                copy_of(kind, d, d).start()

    def receive(kind):
        for d, items in MESSAGES[kind].items():
            back = (-d[0], -d[1])

            @pl.when(there[back])
            def _():
                copy_of(kind, d, back).wait_recv()
                start = PLACES[kind, d][0]
                for item in items:
                    at(item, d)[...] = received[pl.ds(start, item[4]), :]
                    start += item[4]

    def outside(kind):
        for d, items in MESSAGES[kind].items():

            @pl.when(jnp.logical_not(there[-d[0], -d[1]]))
            def _():
                for item in items:
                    value = OPEN if item[0] == COH else 0.0
                    at(item, d)[...] = jnp.full((item[4], 128), value, jnp.float32)

    depth = lax.broadcasted_iota(jnp.int32, (8, 128), 1)

    def deeper(f, n):
        moved = pltpu.roll(f, (-n) % 128, 1)
        return jnp.where((depth < 128 - n) if n > 0 else (depth >= -n), moved, 0.0)

    def view(field, x, y, form):
        start = row(x, y)
        return ext[field, pl.ds(start, 8) if form == "B" else pl.ds(start, 8, stride=PITCH), :]

    def put(field, x, y, form, value):
        start = row(x, y)
        ext[field, pl.ds(start, 8) if form == "B" else pl.ds(start, 8, stride=PITCH), :] = value

    def along(field, x, y, form, axis, first):
        f = [
            view(field, x + (first + k if axis == 0 else 0), y + (first + k if axis == 1 else 0), form)
            for k in range(4)
        ]
        return NEAR * (f[2] - f[1]) + FAR * (f[3] - f[0])

    def forward(field, x, y, form, axis):
        return along(field, x, y, form, axis, -1)

    def backward(field, x, y, form, axis):
        return along(field, x, y, form, axis, -2)

    def forward_z(f):
        return NEAR * (deeper(f, 1) - f) + FAR * (deeper(f, 2) - deeper(f, -1))

    def backward_z(f):
        return NEAR * (f - deeper(f, -1)) + FAR * (deeper(f, 1) - deeper(f, -2))

    loads[0].wait()
    for x in range(8):
        for field, c in ((SXX, 0), (SXY, 3), (SXZ, 4), (SYY, 1), (SYZ, 5)):
            put(field, x, 0, "B", stress[c, x])
    pack(0)
    pl.semaphore_wait(barrier, sum(there[d].astype(jnp.int32) for d in SIDES))
    send(0)
    for kind in range(3):
        outside(kind)

    for load in loads[1:]:
        load.wait()
    place = cells[0]
    column = lax.broadcasted_iota(jnp.int32, (64, 128), 0) == (place // 128)
    spread = jnp.concatenate(
        [jnp.where(column, H * moment[0, 0, pl.ds(c, 1), :], 0.0) for c in range(6)], axis=0
    )
    at_depth = (lax.broadcasted_iota(jnp.int32, (128, 128), 0) == (place % 128)).astype(jnp.float32)
    source[...] = lax.dot_general(
        spread,
        at_depth,
        (((1,), (1,)), ((), ())),
        precision=lax.Precision.HIGHEST,
        preferred_element_type=jnp.float32,
    )
    for x in range(8):
        damping = jnp.where(absorb[x] == 1, SPONGE, 1.0)
        weight[0, x] = damping
        weight[1, x] = H * material[2, x] * damping
        grown = 1.0 - 0.5 * anelastic[1, x]
        weight[2, x] = grown
        put(PP, x, 0, "B", H * grown * material[0, x])
        put(QQ, x, 0, "B", H * grown * material[1, x])
        cohesion = jnp.zeros((8, 128), jnp.float32)
        friction = jnp.zeros((8, 128), jnp.float32)
        for z in range(ZONES):
            inside = zone[x] == z
            cohesion = jnp.where(inside, cohesion_table[z], cohesion)
            friction = jnp.where(inside, friction_table[z], friction)
        put(COH, x, 0, "B", cohesion)
        put(FRI, x, 0, "B", friction)

    ALL = (CXX, CYY, CZZ, CXY, CXZ, CYZ)
    F_STARTS = (-1, 1)

    for step in range(STEPS):
        kind = 3 * step
        if step:
            pack(kind)
            send(kind)
        for x in range(8):
            keep = 0.5 + 0.5 * anelastic[0, x]
            for c, field in enumerate(ALL):
                base = stress[c, x] + source[pl.ds(c * 64 + x * 8, 8), :] - keep * memory[c, x]
                put(field, x, 0, "B", base)
        pack(kind + 1)
        send(kind + 1)
        receive(kind)
        for x in range(8):
            rate_x = (
                forward(SXX, x, 0, "B", 0) + backward(SXY, x, 0, "B", 1) + backward_z(stress[4, x])
            )
            rate_y = (
                backward(SXY, x, 0, "B", 0) + forward(SYY, x, 0, "B", 1) + backward_z(stress[5, x])
            )
            rate_z = (
                backward(SXZ, x, 0, "B", 0) + backward(SYZ, x, 0, "B", 1) + forward_z(stress[2, x])
            )
            damping, push = weight[0, x], weight[1, x]
            for c, (field, rate) in enumerate(((VX, rate_x), (VY, rate_y), (VZ, rate_z))):
                new = velocity[c, x] * damping + push * rate
                velocity[c, x] = new
                put(field, x, 0, "B", new)
        pack(kind + 2)
        send(kind + 2)
        last = step == STEPS - 1
        if last:
            out_velocity = pltpu.make_async_copy(velocity, velocity_out, out_sem.at[0])
            out_velocity.start()
        receive(kind + 1)
        receive(kind + 2)

        def shear_xy(x, y, form):
            return forward(VX, x, y, form, 1) + forward(VY, x, y, form, 0)

        def shear_xz(x, y, form):
            return forward_z(view(VX, x, y, form)) + forward(VZ, x, y, form, 0)

        def shear_yz(x, y, form):
            return forward_z(view(VY, x, y, form)) + forward(VZ, x, y, form, 1)

        def normal(x, y, form):
            return (
                backward(VX, x, y, form, 0),
                backward(VY, x, y, form, 1),
                backward_z(view(VZ, x, y, form)),
            )

        def put_shear(field, x, y, form, value):
            put(field, x, y, form, value if field == TXY else value + deeper(value, -1))

        def keep_centre(k, x, y, form, trial):
            mean = (trial[0] + trial[1] + trial[2]) * (1.0 / 3.0)
            dev = [t - mean for t in trial]
            cohesion = view(COH, x, y, form)
            limit = jnp.maximum(cohesion - view(FRI, x, y, form) * mean, 0.25 * cohesion)
            centre[k, 0] = 0.5 * (dev[0] * dev[0] + dev[1] * dev[1] + dev[2] * dev[2])
            centre[k, 1] = limit
            if k < 8:
                centre[k, 2] = mean
                for c in range(3):
                    centre[k, 3 + c] = dev[c]

        for x in range(8):
            parts = normal(x, 0, "B")
            volume = parts[0] + parts[1] + parts[2]
            lame, modulus = H * material[0, x], H * material[1, x]
            spread_out = lame * volume
            rates = [spread_out + 2.0 * modulus * e for e in parts] + [
                modulus * e
                for e in (shear_xy(x, 0, "B"), shear_xz(x, 0, "B"), shear_yz(x, 0, "B"))
            ]
            grown, decay, share = weight[2, x], anelastic[0, x], anelastic[1, x]
            trial = []
            for c, field in enumerate(ALL):
                trial.append(view(field, x, 0, "B") + grown * rates[c])
                memory[c, x] = decay * memory[c, x] + share * rates[c]
            for c, field in ((3, TXY), (4, UXZ), (5, UYZ)):
                put_shear(field, x, 0, "B", trial[c])
                centre[x, 3 + c] = trial[c]
            keep_centre(x, x, 0, "B", trial[:3])
        if last:
            out_memory = pltpu.make_async_copy(memory, memory_out, out_sem.at[1])
            out_memory.start()
        beyond = [(8, 8, 0, "B")] + [(9 + k, x, 8, "F") for k, x in enumerate(F_STARTS)]
        for k, x, y, form in beyond:
            parts = normal(x, y, form)
            volume = parts[0] + parts[1] + parts[2]
            lame, modulus = view(PP, x, y, form), view(QQ, x, y, form)
            trial = [
                view(field, x, y, form) + lame * volume + 2.0 * modulus * e
                for field, e in zip(ALL, parts)
            ]
            keep_centre(k, x, y, form, trial)
            for field, base, e in (
                (TXY, CXY, shear_xy(x, y, form)),
                (UXZ, CXZ, shear_xz(x, y, form)),
                (UYZ, CYZ, shear_yz(x, y, form)),
            ):
                put_shear(field, x, y, form, view(base, x, y, form) + modulus * e)
        modulus = view(QQ, -1, 0, "B")
        put_shear(TXY, -1, 0, "B", view(CXY, -1, 0, "B") + modulus * shear_xy(-1, 0, "B"))
        put_shear(UXZ, -1, 0, "B", view(CXZ, -1, 0, "B") + modulus * shear_xz(-1, 0, "B"))
        for x in F_STARTS:
            modulus = view(QQ, x, -1, "F")
            put_shear(TXY, x, -1, "F", view(CXY, x, -1, "F") + modulus * shear_xy(x, -1, "F"))
            put_shear(UYZ, x, -1, "F", view(CYZ, x, -1, "F") + modulus * shear_yz(x, -1, "F"))

        for k, x, y, form in [(x, x, 0, "B") for x in range(8)] + beyond:
            mean_xy = 0.25 * (
                (view(TXY, x - 1, y - 1, form) + view(TXY, x - 1, y, form))
                + (view(TXY, x, y - 1, form) + view(TXY, x, y, form))
            )
            mean_xz = 0.25 * (view(UXZ, x - 1, y, form) + view(UXZ, x, y, form))
            mean_yz = 0.25 * (view(UYZ, x, y - 1, form) + view(UYZ, x, y, form))
            tau = jnp.sqrt(
                centre[k, 0] + mean_xy * mean_xy + mean_xz * mean_xz + mean_yz * mean_yz
            )
            ratio = jnp.minimum(1.0, centre[k, 1] / jnp.maximum(tau, 0.5))
            deficit = 1.0 - ratio
            put(DEF, x, y, form, deficit)
            put(DEZ, x, y, form, deficit + deeper(deficit, 1))
            if k < 8:
                centre[k, 1] = ratio

        for x in range(8):
            ratio, mean = centre[x, 1], centre[x, 2]
            new = [mean + ratio * centre[x, 3 + c] for c in range(3)]
            lack = [view(DEF, x + i, j, "B") for i in (0, 1) for j in (0, 1)]
            new.append((1.0 - 0.25 * ((lack[0] + lack[1]) + (lack[2] + lack[3]))) * centre[x, 6])
            here = view(DEZ, x, 0, "B")
            new.append((1.0 - 0.25 * (here + view(DEZ, x + 1, 0, "B"))) * centre[x, 7])
            new.append((1.0 - 0.25 * (here + view(DEZ, x, 1, "B"))) * centre[x, 8])
            for c in range(6):
                stress[c, x] = new[c]
            if not last:
                for field, c in ((SXX, 0), (SXY, 3), (SXZ, 4), (SYY, 1), (SYZ, 5)):
                    put(field, x, 0, "B", new[c])

    out_stress = pltpu.make_async_copy(stress, stress_out, out_sem.at[2])
    out_stress.start()
    for kind, table in enumerate(MESSAGES):
        for d in table:

            @pl.when(there[d])
            def _():
                copy_of(kind, d, d).wait_send()

    out_velocity.wait()
    out_memory.wait()
    out_stress.wait()


def shards(
    n_gx,
    n_gy,
    velocity,
    stress,
    memory,
    material,
    anelastic,
    zone_ids,
    absorb_mask,
    source_cells,
    source_moment,
    cohesion_table,
    friction_table,
):
    whole = pl.BlockSpec(memory_space=pl.ANY)
    table = pl.BlockSpec(memory_space=pltpu.SMEM)
    f32, i32 = jnp.float32, jnp.int32
    block = (8, 8, 128)
    return tuple(
        pl.pallas_call(
            functools.partial(kernel, n_gx, n_gy),
            out_shape=[
                jax.ShapeDtypeStruct((3, *block), f32),
                jax.ShapeDtypeStruct((6, *block), f32),
                jax.ShapeDtypeStruct((6, *block), f32),
            ],
            in_specs=[whole] * 9 + [table] * 2,
            out_specs=[whole] * 3,
            scratch_shapes=[
                pltpu.VMEM((FIELDS, SLABS * PITCH, 128), f32),
                pltpu.VMEM((BUFFER_ROWS, 128), f32),
                pltpu.VMEM((BUFFER_ROWS, 128), f32),
                pltpu.VMEM((3, *block), f32),
                pltpu.VMEM((6, *block), f32),
                pltpu.VMEM((6, *block), f32),
                pltpu.VMEM((3, *block), f32),
                pltpu.VMEM((2, *block), f32),
                pltpu.VMEM(block, i32),
                pltpu.VMEM(block, i32),
                pltpu.VMEM((1, 1, 128), i32),
                pltpu.VMEM((1, 1, 6, 128), f32),
                pltpu.VMEM((6 * 64, 128), f32),
                pltpu.VMEM((3, *block), f32),
                pltpu.VMEM((11, 9, 8, 128), f32),
                pltpu.SemaphoreType.DMA((N_MESSAGES,)),
                pltpu.SemaphoreType.DMA((N_MESSAGES,)),
                pltpu.SemaphoreType.DMA((9,)),
                pltpu.SemaphoreType.DMA((3,)),
            ],
            compiler_params=pltpu.CompilerParams(
                collective_id=0, has_side_effects=True, vmem_limit_bytes=48 * 2**20
            ),
            name="waves",
        )(
            velocity,
            stress,
            memory,
            material,
            anelastic,
            zone_ids,
            absorb_mask,
            source_cells,
            source_moment,
            cohesion_table,
            friction_table,
        )
    )


def solution(mesh):
    in_specs = (
        P(None, "gx", "gy", None),
        P(None, "gx", "gy", None),
        P(None, "gx", "gy", None),
        P(None, "gx", "gy", None),
        P(None, "gx", "gy", None),
        P("gx", "gy", None),
        P("gx", "gy", None),
        P("gx", "gy", None),
        P("gx", "gy", None, None),
        P(),
        P(),
    )
    out_specs = (P(None, "gx", "gy", None), P(None, "gx", "gy", None), P(None, "gx", "gy", None))
    body = functools.partial(shards, mesh.shape["gx"], mesh.shape["gy"])
    return jax.shard_map(body, mesh=mesh, in_specs=in_specs, out_specs=out_specs, check_vma=False)
```

time: 234 us -> 43.2 us (0.18)
  the two profiles are of different devices: /device:TPU:534 before, /device:TPU:1 now
where the time goes in v1:
time: 43.2 us; the launch traced here: 42.8 us
  Pallas kernels  33.4 us (77%)
  local copies, waits for them, and re-layouts  8.7 us (20%)
  between operations  0.68 us (2%)
    pallas_call x1, Pallas kernels, shards(): pl.pallas_call(functools.partial(kernel, n_gx, n_gy), out_shape=[jax.Shap...  33.4 us
    unnamed x24, local copies, waits for them, and re-layouts  8.7 us

profile of v1, /device:TPU:1, one launch (start us, length us, event | category | flops | bytes accessed | tf_op | source)
XLA Modules:
  0.0 42.8 jit_solution(10976983082575172843)
XLA Ops:
  0.6 0.0 copy-start.9
  0.6 0.0 copy-start.8
  0.7 0.0 copy-start.7
  0.7 0.7 %copy.14.moment_in = f32[1,1,6,128]{3,2,1,0:T(8,128)S(1)} copy(f32[1,1,6,128]{3,1,2,0:T(1,128)} %param.19) | data formatting | bytes 6144 | tf_op args[8]
  1.4 0.0 copy-done.9
  1.4 0.0 copy-done.8
  1.4 0.0 copy-done.7
  1.4 0.0 copy-start
  1.4 0.9 %copy-done = f32[6,8,8,128]{3,2,1,0:T(8,128)S(1)} copy-done((f32[6,8,8,128]{3,2,1,0:T(8,128)S(1)}, f32[6,8,8,128]{3,2,1,0:T(8,128)}, u32[]{:S(2)}) %copy-start) | copy-done | bytes 196632
  2.3 0.0 copy-start.1
  2.3 0.9 %copy-done.1 = f32[6,8,8,128]{3,2,1,0:T(8,128)S(1)} copy-done((f32[6,8,8,128]{3,2,1,0:T(8,128)S(1)}, f32[6,8,8,128]{3,2,1,0:T(8,128)}, u32[]{:S(2)}) %copy-start.1) | copy-done | bytes 196632
  3.2 0.0 copy-start.2
  3.2 0.9 %copy-done.2 = f32[3,8,8,128]{3,2,1,0:T(8,128)S(1)} copy-done((f32[3,8,8,128]{3,2,1,0:T(8,128)S(1)}, f32[3,8,8,128]{3,2,1,0:T(8,128)}, u32[]{:S(2)}) %copy-start.2) | copy-done | bytes 98328
  4.1 0.0 copy-start.3
  4.1 0.9 %copy-done.3 = f32[3,8,8,128]{3,2,1,0:T(8,128)S(1)} copy-done((f32[3,8,8,128]{3,2,1,0:T(8,128)S(1)}, f32[3,8,8,128]{3,2,1,0:T(8,128)}, u32[]{:S(2)}) %copy-start.3) | copy-done | bytes 98328
  5.0 0.0 copy-start.4
  5.0 0.8 %copy-done.4 = f32[2,8,8,128]{3,2,1,0:T(8,128)S(1)} copy-done((f32[2,8,8,128]{3,2,1,0:T(8,128)S(1)}, f32[2,8,8,128]{3,2,1,0:T(8,128)}, u32[]{:S(2)}) %copy-start.4) | copy-done | bytes 65560
  5.9 0.0 copy-start.5
  5.9 0.8 %copy-done.5 = s32[8,8,128]{2,1,0:T(8,128)S(1)} copy-done((s32[8,8,128]{2,1,0:T(8,128)S(1)}, s32[8,8,128]{2,1,0:T(8,128)}, u32[]{:S(2)}) %copy-start.5) | copy-done | bytes 32792
  6.6 0.0 copy-start.6
  6.6 0.8 %copy-done.6 = s32[8,8,128]{2,1,0:T(8,128)S(1)} copy-done((s32[8,8,128]{2,1,0:T(8,128)S(1)}, s32[8,8,128]{2,1,0:T(8,128)}, u32[]{:S(2)}) %copy-start.6) | copy-done | bytes 32792
  7.4 33.4 %waves.1 = (f32[3,8,8,128]{3,2,1,0:T(8,128)S(1)}, f32[6,8,8,128]{3,2,1,0:T(8,128)S(1)}, f32[6,8,8,128]{3,2,1,0:T(8,128)S(1)}) custom-call(f32[3,8,8,128]{3,2,1,0:T(8,128)S(1)} %copy-done.2, f32[6,8,8,128]{3,2,1,0:T(8,128)S(1)} %copy-done, f32[6,8,8,128]{3,2,1,0:T(8,128)S(1)} %copy-done.1, f32[3,8,8,128]{3,2,1,0:T(8,128)S(1)} %copy-done.3, ...), custom_call_target="tpu_custom_call" | custom-call | tf_op jit(solution)/shard_map/waves/pallas_call | solution.py:516
  40.8 0.6 %copy.18 = f32[3,8,8,128]{3,2,1,0:T(8,128)} copy(f32[3,8,8,128]{3,2,1,0:T(8,128)S(1)} %get-tuple-element.6) | data formatting | bytes 196608
  41.4 0.7 %copy.19 = f32[6,8,8,128]{3,2,1,0:T(8,128)} copy(f32[6,8,8,128]{3,2,1,0:T(8,128)S(1)} %get-tuple-element.7) | data formatting | bytes 393216
  42.1 0.7 %copy.20 = f32[6,8,8,128]{3,2,1,0:T(8,128)} copy(f32[6,8,8,128]{3,2,1,0:T(8,128)S(1)} %get-tuple-element.8) | data formatting | bytes 393216
Async XLA Ops:
  0.6 0.7 %copy-start.9 = (f32[8]{0:T(128)S(1)}, f32[8]{0:T(128)}, u32[]{:S(2)}) copy-start(f32[8]{0:T(128)} %friction_table.1) | copy-start | bytes 100
  0.6 0.7 %copy-start.8 = (f32[8]{0:T(128)S(1)}, f32[8]{0:T(128)}, u32[]{:S(2)}) copy-start(f32[8]{0:T(128)} %cohesion_table.1) | copy-start | bytes 100
  0.7 0.7 %copy-start.7 = (s32[1,1,128]{2,1,0:T(1,128)S(1)}, s32[1,1,128]{2,1,0:T(1,128)}, u32[]{:S(2)}) copy-start(s32[1,1,128]{2,1,0:T(1,128)} %cells_in.1) | copy-start | bytes 1540
  1.4 0.9 %copy-start = (f32[6,8,8,128]{3,2,1,0:T(8,128)S(1)}, f32[6,8,8,128]{3,2,1,0:T(8,128)}, u32[]{:S(2)}) copy-start(f32[6,8,8,128]{3,2,1,0:T(8,128)} %stress_in.1) | copy-start | bytes 589828
  2.3 0.9 %copy-start.1 = (f32[6,8,8,128]{3,2,1,0:T(8,128)S(1)}, f32[6,8,8,128]{3,2,1,0:T(8,128)}, u32[]{:S(2)}) copy-start(f32[6,8,8,128]{3,2,1,0:T(8,128)} %memory_in.1) | copy-start | bytes 589828
  3.2 0.9 %copy-start.2 = (f32[3,8,8,128]{3,2,1,0:T(8,128)S(1)}, f32[3,8,8,128]{3,2,1,0:T(8,128)}, u32[]{:S(2)}) copy-start(f32[3,8,8,128]{3,2,1,0:T(8,128)} %velocity_in.1) | copy-start | bytes 294916
  4.1 0.9 %copy-start.3 = (f32[3,8,8,128]{3,2,1,0:T(8,128)S(1)}, f32[3,8,8,128]{3,2,1,0:T(8,128)}, u32[]{:S(2)}) copy-start(f32[3,8,8,128]{3,2,1,0:T(8,128)} %material_in.1) | copy-start | bytes 294916
  5.0 0.8 %copy-start.4 = (f32[2,8,8,128]{3,2,1,0:T(8,128)S(1)}, f32[2,8,8,128]{3,2,1,0:T(8,128)}, u32[]{:S(2)}) copy-start(f32[2,8,8,128]{3,2,1,0:T(8,128)} %anelastic_in.1) | copy-start | bytes 196612
  5.9 0.8 %copy-start.5 = (s32[8,8,128]{2,1,0:T(8,128)S(1)}, s32[8,8,128]{2,1,0:T(8,128)}, u32[]{:S(2)}) copy-start(s32[8,8,128]{2,1,0:T(8,128)} %zone_in.1) | copy-start | bytes 98308
  6.6 0.8 %copy-start.6 = (s32[8,8,128]{2,1,0:T(8,128)S(1)}, s32[8,8,128]{2,1,0:T(8,128)}, u32[]{:S(2)}) copy-start(s32[8,8,128]{2,1,0:T(8,128)} %absorb_in.1) | copy-start | bytes 98308

commit v2 on v1

--- a/solution.py
+++ b/solution.py
@@ -144,30 +144,28 @@
     absorb_in,
     cells_in,
     moment_in,
-    cohesion_table,
-    friction_table,
-    velocity_out,
-    stress_out,
-    memory_out,
+    cohesion_in,
+    friction_in,
+    velocity,
+    stress,
+    memory,
     ext,
     sent,
     received,
-    velocity,
-    stress,
-    memory,
     material,
     anelastic,
     zone,
     absorb,
     cells,
     moment,
+    cohesion_table,
+    friction_table,
     source,
     weight,
     centre,
     send_sem,
     recv_sem,
     in_sem,
-    out_sem,
 ):
     gx, gy = lax.axis_index("gx"), lax.axis_index("gy")
     there = {}
@@ -201,6 +199,8 @@
             (absorb_in, absorb),
             (cells_in, cells),
             (moment_in, moment),
+            (cohesion_in, cohesion_table),
+            (friction_in, friction_table),
         )
     ):
         loads.append(pltpu.make_async_copy(src, dst, in_sem.at[k]))
@@ -305,7 +305,7 @@
     place = cells[0]
     column = lax.broadcasted_iota(jnp.int32, (64, 128), 0) == (place // 128)
     spread = jnp.concatenate(
-        [jnp.where(column, H * moment[0, 0, pl.ds(c, 1), :], 0.0) for c in range(6)], axis=0
+        [jnp.where(column, H * moment[0, c], 0.0) for c in range(6)], axis=0
     )
     at_depth = (lax.broadcasted_iota(jnp.int32, (128, 128), 0) == (place % 128)).astype(jnp.float32)
     source[...] = lax.dot_general(
@@ -366,9 +366,6 @@
         pack(kind + 2)
         send(kind + 2)
         last = step == STEPS - 1
-        if last:
-            out_velocity = pltpu.make_async_copy(velocity, velocity_out, out_sem.at[0])
-            out_velocity.start()
         receive(kind + 1)
         receive(kind + 2)
 
@@ -421,9 +418,6 @@
                 put_shear(field, x, 0, "B", trial[c])
                 centre[x, 3 + c] = trial[c]
             keep_centre(x, x, 0, "B", trial[:3])
-        if last:
-            out_memory = pltpu.make_async_copy(memory, memory_out, out_sem.at[1])
-            out_memory.start()
         beyond = [(8, 8, 0, "B")] + [(9 + k, x, 8, "F") for k, x in enumerate(F_STARTS)]
         for k, x, y, form in beyond:
             parts = normal(x, y, form)
@@ -479,8 +473,6 @@
                 for field, c in ((SXX, 0), (SXY, 3), (SXZ, 4), (SYY, 1), (SYZ, 5)):
                     put(field, x, 0, "B", new[c])
 
-    out_stress = pltpu.make_async_copy(stress, stress_out, out_sem.at[2])
-    out_stress.start()
     for kind, table in enumerate(MESSAGES):
         for d in table:
 
@@ -488,9 +480,14 @@
             def _():
                 copy_of(kind, d, d).wait_send()
 
-    out_velocity.wait()
-    out_memory.wait()
-    out_stress.wait()
+
+def hand_over(*refs):
+    n = (len(refs) - 1) // 2
+    copies = [pltpu.make_async_copy(refs[k], refs[n + k], refs[-1].at[k]) for k in range(n)]
+    for copy in copies:
+        copy.start()
+    for copy in copies:
+        copy.wait()
 
 
 def shards(
@@ -508,58 +505,61 @@
     cohesion_table,
     friction_table,
 ):
-    whole = pl.BlockSpec(memory_space=pl.ANY)
-    table = pl.BlockSpec(memory_space=pltpu.SMEM)
+    far = pl.BlockSpec(memory_space=pl.ANY)
+    near = pl.BlockSpec(memory_space=pltpu.VMEM)
     f32, i32 = jnp.float32, jnp.int32
     block = (8, 8, 128)
+    operands = (
+        velocity,
+        stress,
+        memory,
+        material,
+        anelastic,
+        zone_ids,
+        absorb_mask,
+        source_cells,
+        jnp.swapaxes(source_moment, 1, 2),
+        cohesion_table,
+        friction_table,
+    )
+    results = pl.pallas_call(
+        functools.partial(kernel, n_gx, n_gy),
+        out_shape=[pltpu.VMEM((n, *block), f32) for n in (3, 6, 6)],
+        in_specs=[far] * 11,
+        out_specs=[near] * 3,
+        scratch_shapes=[
+            pltpu.VMEM((FIELDS, SLABS * PITCH, 128), f32),
+            pltpu.VMEM((BUFFER_ROWS, 128), f32),
+            pltpu.VMEM((BUFFER_ROWS, 128), f32),
+            pltpu.VMEM((3, *block), f32),
+            pltpu.VMEM((2, *block), f32),
+            pltpu.VMEM(block, i32),
+            pltpu.VMEM(block, i32),
+            pltpu.VMEM((1, 1, 128), i32),
+            pltpu.VMEM((1, 6, 1, 128), f32),
+            pltpu.SMEM((ZONES,), f32),
+            pltpu.SMEM((ZONES,), f32),
+            pltpu.VMEM((6 * 64, 128), f32),
+            pltpu.VMEM((3, *block), f32),
+            pltpu.VMEM((11, 9, 8, 128), f32),
+            pltpu.SemaphoreType.DMA((N_MESSAGES,)),
+            pltpu.SemaphoreType.DMA((N_MESSAGES,)),
+            pltpu.SemaphoreType.DMA((11,)),
+        ],
+        compiler_params=pltpu.CompilerParams(
+            collective_id=0, has_side_effects=True, vmem_limit_bytes=32 * 2**20
+        ),
+        name="waves",
+    )(*[pltpu.with_memory_space_constraint(x, pltpu.HBM) for x in operands])
     return tuple(
         pl.pallas_call(
-            functools.partial(kernel, n_gx, n_gy),
-            out_shape=[
-                jax.ShapeDtypeStruct((3, *block), f32),
-                jax.ShapeDtypeStruct((6, *block), f32),
-                jax.ShapeDtypeStruct((6, *block), f32),
-            ],
-            in_specs=[whole] * 9 + [table] * 2,
-            out_specs=[whole] * 3,
-            scratch_shapes=[
-                pltpu.VMEM((FIELDS, SLABS * PITCH, 128), f32),
-                pltpu.VMEM((BUFFER_ROWS, 128), f32),
-                pltpu.VMEM((BUFFER_ROWS, 128), f32),
-                pltpu.VMEM((3, *block), f32),
-                pltpu.VMEM((6, *block), f32),
-                pltpu.VMEM((6, *block), f32),
-                pltpu.VMEM((3, *block), f32),
-                pltpu.VMEM((2, *block), f32),
-                pltpu.VMEM(block, i32),
-                pltpu.VMEM(block, i32),
-                pltpu.VMEM((1, 1, 128), i32),
-                pltpu.VMEM((1, 1, 6, 128), f32),
-                pltpu.VMEM((6 * 64, 128), f32),
-                pltpu.VMEM((3, *block), f32),
-                pltpu.VMEM((11, 9, 8, 128), f32),
-                pltpu.SemaphoreType.DMA((N_MESSAGES,)),
-                pltpu.SemaphoreType.DMA((N_MESSAGES,)),
-                pltpu.SemaphoreType.DMA((9,)),
-                pltpu.SemaphoreType.DMA((3,)),
-            ],
-            compiler_params=pltpu.CompilerParams(
-                collective_id=0, has_side_effects=True, vmem_limit_bytes=48 * 2**20
-            ),
-            name="waves",
-        )(
-            velocity,
-            stress,
-            memory,
-            material,
-            anelastic,
-            zone_ids,
-            absorb_mask,
-            source_cells,
-            source_moment,
-            cohesion_table,
-            friction_table,
-        )
+            hand_over,
+            out_shape=[jax.ShapeDtypeStruct(r.shape, r.dtype) for r in results],
+            in_specs=[near] * 3,
+            out_specs=[far] * 3,
+            scratch_shapes=[pltpu.SemaphoreType.DMA((3,))],
+            name="results",
+        )(*[pltpu.with_memory_space_constraint(r, pltpu.VMEM) for r in results])
     )
 
 

time: 43.2 us -> 33.8 us (0.78)
  local copies, waits for them, and re-layouts: 8.7 us -> 0 us
  Pallas kernels: 33.4 us -> 32.9 us
    unnamed x24 -> x0, local copies, waits for them, and re-layouts: 8.7 us -> none
    pallas_call x1 -> x2, Pallas kernels: 33.4 us -> 32.9 us  [the longest x1 32.1 us: shards(): pl.pallas_call(functools.partial(kernel, n_gx, n_gy), out_shape=[pltpu.VM...]
where the time goes in v2:
time: 33.8 us; the launch traced here: 33.6 us
  Pallas kernels  32.9 us (97%)
  between operations  0.64 us (2%)
    pallas_call x1, Pallas kernels, shards(): pl.pallas_call(functools.partial(kernel, n_gx, n_gy), out_shape=[pltpu.VM...  32.1 us
    pallas_call x1, Pallas kernels, shards(): pl.pallas_call(hand_over, out_shape=[jax.ShapeDtypeStruct(r.shape, r.dtyp...  0.8 us

profile of v2, /device:TPU:1, one launch (start us, length us, event | category | flops | bytes accessed | tf_op | source)
XLA Modules:
  0.0 33.6 jit_solution(10511256629144191675)
XLA Ops:
  0.6 32.1 %waves.1 = (f32[3,8,8,128]{3,2,1,0:T(8,128)S(1)}, f32[6,8,8,128]{3,2,1,0:T(8,128)S(1)}, f32[6,8,8,128]{3,2,1,0:T(8,128)S(1)}) custom-call(f32[3,8,8,128]{3,2,1,0:T(8,128)} %velocity_in.1, f32[6,8,8,128]{3,2,1,0:T(8,128)} %stress_in.1, f32[6,8,8,128]{3,2,1,0:T(8,128)} %memory_in.1, f32[3,8,8,128]{3,2,1,0:T(8,128)} %material_in.1, ...), custom_call_target="tpu_custom_call" | custom-call | tf_op jit(solution)/shard_map/waves/pallas_call | solution.py:525
  32.8 0.8 %results.1 = (f32[3,8,8,128]{3,2,1,0:T(8,128)}, f32[6,8,8,128]{3,2,1,0:T(8,128)}, f32[6,8,8,128]{3,2,1,0:T(8,128)}) custom-call(f32[3,8,8,128]{3,2,1,0:T(8,128)S(1)} %get-tuple-element.6.refs_0_, f32[6,8,8,128]{3,2,1,0:T(8,128)S(1)} %get-tuple-element.7.refs_1_, f32[6,8,8,128]{3,2,1,0:T(8,128)S(1)} %get-tuple-element.8.refs_2_), custom_call_target="tpu_custom_call" | custom-call | tf_op jit(solution)/shard_map/results/pallas_call | solution.py:555

commit v3 on v2

--- a/solution.py
+++ b/solution.py
@@ -16,11 +16,11 @@
 SPONGE = 0.92
 OPEN = 1.0e9
 
-SXX, SXY, SXZ, SYY, SYZ, VX, VY, VZ = range(8)
-CXX, CYY, CZZ, CXY, CXZ, CYZ = range(8, 14)
-PP, QQ, COH, FRI = range(14, 18)
-TXY, UXZ, UYZ, DEF, DEZ = range(18, 23)
-FIELDS = 23
+SXX, SXY, SXZ, SYY, SYZ, VX, VY, VZ, RX, RY, RZ = range(11)
+CXX, CYY, CZZ, CXY, CXZ, CYZ = range(11, 17)
+PP, QQ, COH, FRI, PUSH = range(17, 22)
+TXY, UXZ, UYZ, DEF, DEZ = range(22, 27)
+FIELDS = 27
 SLABS = 14
 PITCH = 16
 
@@ -45,82 +45,77 @@
     return (field, "B", x, y, n)
 
 
-STRESS_SENT = {
-    (1, 0): [xs(SXX, 7), xs(SXY, 6), xs(SXY, 7), xs(SXZ, 6), xs(SXZ, 7)],
-    (-1, 0): [xs(SXX, 0), xs(SXX, 1), xs(SXY, 0), xs(SXZ, 0)],
-    (0, 1): [ys(SYY, 7), ys(SXY, 6), ys(SXY, 7), ys(SYZ, 6), ys(SYZ, 7)],
-    (0, -1): [ys(SYY, 0), ys(SYY, 1), ys(SXY, 0), ys(SYZ, 0)],
+def boxes(*parts):
+    return [some(f, x, y, n) for f, x, y, n in parts]
+
+
+def rows_x(field, *at):
+    return [xs(field, x) for x in at]
+
+
+def rows_y(field, *at):
+    return [ys(field, y) for y in at]
+
+
+NORMAL_AND_SHEAR = (CXX, CYY, CZZ, CXY, CXZ, CYZ)
+
+EACH_STEP = {
+    (1, 0): rows_x(VX, 6, 7) + rows_x(VY, 6, 7) + rows_x(VZ, 6, 7)
+    + rows_x(RX, 8) + rows_x(RY, 8, 9) + rows_x(RZ, 8, 9) + rows_x(CXY, 7) + rows_x(CXZ, 7)
+    + boxes((RX, 7, 8, 2), (RX, 6, 8, 1), (RY, 6, 8, 1), (RY, 7, 8, 1), (RZ, 6, 8, 1), (RZ, 7, 8, 1))
+    + boxes((RX, 7, -1, 1), (RY, 6, -1, 1), (RY, 7, -1, 1)),
+    (-1, 0): rows_x(VX, 0, 1) + rows_x(VY, 0, 1, 2) + rows_x(VZ, 0, 1, 2)
+    + rows_x(RX, -2, -1) + rows_x(RY, -1) + rows_x(RZ, -1)
+    + [xs(f, 0) for f in NORMAL_AND_SHEAR]
+    + boxes((RX, 0, 8, 2), (RX, 1, 8, 1), (RY, 0, 8, 1), (RY, 1, 8, 1), (RY, 2, 8, 1))
+    + boxes((RZ, 0, 8, 2), (RZ, 1, 8, 1), (RZ, 2, 8, 1))
+    + boxes((RX, 0, -1, 1), (RY, 0, -2, 2), (RY, 1, -1, 1), (RY, 2, -1, 1), (RZ, 0, -1, 1)),
+    (0, 1): rows_y(VX, 6, 7) + rows_y(VY, 6, 7) + rows_y(VZ, 6, 7)
+    + rows_y(RY, 8) + rows_y(RX, 8, 9) + rows_y(RZ, 8, 9) + rows_y(CXY, 7) + rows_y(CYZ, 7)
+    + boxes((RX, 8, 6, 2), (RY, 8, 6, 2), (RY, 9, 7, 1), (RZ, 8, 6, 2))
+    + boxes((RX, -1, 6, 2), (RY, -1, 7, 1)),
+    (0, -1): rows_y(VY, 0, 1) + rows_y(VX, 0, 1, 2) + rows_y(VZ, 0, 1, 2)
+    + rows_y(RY, -2, -1) + rows_y(RX, -1) + rows_y(RZ, -1)
+    + [ys(f, 0) for f in NORMAL_AND_SHEAR]
+    + boxes((RX, 8, 0, 3), (RY, 8, 0, 2), (RY, 9, 0, 1), (RZ, 8, 0, 3), (RZ, 9, 0, 1))
+    + boxes((RX, -1, 0, 3), (RX, -2, 0, 1), (RY, -1, 0, 1), (RZ, -1, 0, 1)),
+    (1, 1): boxes((VX, 7, 6, 2), (VY, 6, 7, 1), (VY, 7, 7, 1), (CXY, 7, 7, 1))
+    + boxes((RX, 6, 8, 2), (RX, 7, 8, 2), (RY, 6, 8, 1), (RY, 7, 8, 1), (RZ, 6, 8, 2), (RZ, 7, 8, 2))
+    + boxes((RX, 8, 6, 2), (RY, 8, 6, 2), (RY, 9, 6, 2), (RZ, 8, 6, 2), (RZ, 9, 6, 2)),
+    (-1, -1): boxes((VX, 0, 0, 3), (VX, 1, 0, 1), (VY, 0, 0, 2), (VY, 1, 0, 1), (VY, 2, 0, 1))
+    + boxes((VZ, 0, 0, 3), (VZ, 1, 0, 1), (VZ, 2, 0, 1))
+    + [some(f, 0, 0) for f in NORMAL_AND_SHEAR]
+    + boxes((RX, 0, -1, 1), (RX, 1, -1, 1), (RY, 0, -2, 2), (RY, 1, -2, 2), (RY, 2, -2, 2))
+    + boxes((RZ, 0, -1, 1), (RZ, 1, -1, 1), (RZ, 2, -1, 1))
+    + boxes((RX, -2, 0, 3), (RX, -1, 0, 3), (RY, -1, 0, 2), (RZ, -1, 0, 3)),
+    (-1, 1): boxes((VX, 0, 6, 2), (VY, 0, 6, 2), (VY, 1, 7, 1), (VY, 2, 7, 1), (VZ, 0, 6, 2))
+    + boxes((CXY, 0, 7, 1), (CYZ, 0, 7, 1))
+    + boxes((RX, 0, 8, 2), (RX, 1, 8, 2), (RY, 0, 8, 1), (RY, 1, 8, 1), (RY, 2, 8, 1))
+    + boxes((RZ, 0, 8, 2), (RZ, 1, 8, 2), (RZ, 2, 8, 2))
+    + boxes((RX, -2, 6, 2), (RX, -1, 6, 2), (RY, -1, 6, 2), (RZ, -1, 6, 2)),
+    (1, -1): boxes((VX, 7, 0, 3), (VX, 6, 0, 1), (VY, 6, 0, 1), (VY, 7, 0, 1), (VZ, 6, 0, 1), (VZ, 7, 0, 1))
+    + boxes((CXY, 7, 0, 1), (CXZ, 7, 0, 1))
+    + boxes((RX, 6, -1, 1), (RX, 7, -1, 1), (RY, 6, -2, 2), (RY, 7, -2, 2), (RZ, 6, -1, 1), (RZ, 7, -1, 1))
+    + boxes((RX, 8, 0, 3), (RY, 8, 0, 2), (RY, 9, 0, 2), (RZ, 8, 0, 3), (RZ, 9, 0, 3)),
 }
-BASE_SENT = {
-    (1, 0): [xs(CXY, 7), xs(CXZ, 7)],
-    (-1, 0): [xs(f, 0) for f in (CXX, CYY, CZZ, CXY, CXZ, CYZ)],
-    (0, 1): [ys(CXY, 7), ys(CYZ, 7)],
-    (0, -1): [ys(f, 0) for f in (CXX, CYY, CZZ, CXY, CXZ, CYZ)],
+ONCE = {
+    (1, 0): rows_x(QQ, 7) + rows_x(PUSH, 6, 7),
+    (-1, 0): [xs(f, 0) for f in (PP, QQ, COH, FRI)] + rows_x(PUSH, 0, 1, 2),
+    (0, 1): rows_y(QQ, 7) + rows_y(PUSH, 6, 7),
+    (0, -1): [ys(f, 0) for f in (PP, QQ, COH, FRI)] + rows_y(PUSH, 0, 1, 2),
+    (1, 1): boxes((QQ, 7, 7, 1), (PUSH, 7, 6, 2), (PUSH, 6, 7, 1)),
+    (-1, -1): [some(f, 0, 0) for f in (PP, QQ, COH, FRI)]
+    + boxes((PUSH, 0, 0, 3), (PUSH, 1, 0, 1), (PUSH, 2, 0, 1)),
+    (-1, 1): boxes((QQ, 0, 7, 1), (PUSH, 0, 6, 2), (PUSH, 1, 7, 1), (PUSH, 2, 7, 1)),
+    (1, -1): boxes((QQ, 7, 0, 1), (PUSH, 7, 0, 3), (PUSH, 6, 0, 1)),
 }
-FIXED_SENT = {
-    (1, 0): [xs(QQ, 7)],
-    (-1, 0): [xs(f, 0) for f in (PP, QQ, COH, FRI)],
-    (0, 1): [ys(QQ, 7)],
-    (0, -1): [ys(f, 0) for f in (PP, QQ, COH, FRI)],
-    (1, 1): [some(QQ, 7, 7)],
-    (-1, -1): [some(f, 0, 0) for f in (PP, QQ, COH, FRI)],
-    (-1, 1): [some(QQ, 0, 7)],
-    (1, -1): [some(QQ, 7, 0)],
-}
-VELOCITY_SENT = {
-    (1, 0): [xs(f, x) for f in (VX, VY, VZ) for x in (6, 7)],
-    (-1, 0): [xs(f, x) for f, n in ((VX, 2), (VY, 3), (VZ, 3)) for x in range(n)],
-    (0, 1): [ys(f, y) for f in (VX, VY, VZ) for y in (6, 7)],
-    (0, -1): [ys(f, y) for f, n in ((VX, 3), (VY, 2), (VZ, 3)) for y in range(n)],
-    (1, 1): [some(VX, 7, 6, 2), some(VY, 6, 7), some(VY, 7, 7), some(CXY, 7, 7)],
-    (-1, -1): [
-        some(VX, 0, 0, 3),
-        some(VX, 1, 0),
-        some(VY, 0, 0, 2),
-        some(VY, 1, 0),
-        some(VY, 2, 0),
-        some(VZ, 0, 0, 3),
-        some(VZ, 1, 0),
-        some(VZ, 2, 0),
-    ]
-    + [some(f, 0, 0) for f in (CXX, CYY, CZZ, CXY, CXZ, CYZ)],
-    (-1, 1): [
-        some(VX, 0, 6, 2),
-        some(VY, 0, 6, 2),
-        some(VY, 1, 7),
-        some(VY, 2, 7),
-        some(VZ, 0, 6, 2),
-        some(CXY, 0, 7),
-        some(CYZ, 0, 7),
-    ],
-    (1, -1): [
-        some(VX, 7, 0, 3),
-        some(VX, 6, 0),
-        some(VY, 6, 0),
-        some(VY, 7, 0),
-        some(VZ, 6, 0),
-        some(VZ, 7, 0),
-        some(CXY, 7, 0),
-        some(CXZ, 7, 0),
-    ],
-}
-
-
-def joined(*tables):
-    return {d: sum((t.get(d, []) for t in tables), []) for d in SIDES if any(d in t for t in tables)}
 
 
 def rows_of(items):
     return -(-sum(item[4] for item in items) // 8) * 8
 
 
-MESSAGES = []
-for first in (True, False):
-    MESSAGES.append(STRESS_SENT)
-    faces_fixed = {d: FIXED_SENT[d] for d in FACES}
-    MESSAGES.append(joined(BASE_SENT, faces_fixed) if first else BASE_SENT)
-    corners_fixed = {d: FIXED_SENT[d] for d in CORNERS}
-    MESSAGES.append(joined(VELOCITY_SENT, corners_fixed) if first else VELOCITY_SENT)
+MESSAGES = [{d: ONCE[d] + EACH_STEP[d] for d in SIDES}, EACH_STEP]
 
 PLACES = {}
 used = 0
@@ -206,10 +201,16 @@
         loads.append(pltpu.make_async_copy(src, dst, in_sem.at[k]))
         loads[-1].start()
 
-    def at(item, d=(0, 0)):
+    def spot(field, form, x, y, n):
+        start = row(x, y)
+        return ext.at[field, pl.ds(start, n) if form == "B" else pl.ds(start, n, stride=PITCH), :]
+
+    def at(item):
+        return spot(*item)
+
+    def landed(item, d):
         field, form, x, y, n = item
-        start = row(x - 8 * d[0], y - 8 * d[1])
-        return ext.at[field, pl.ds(start, n) if form == "B" else pl.ds(start, n, stride=PITCH), :]
+        return (field, form, x - 8 * d[0], y - 8 * d[1], n)
 
     def copy_of(kind, d, sem_side):
         start, n, k = PLACES[kind, d]
@@ -245,8 +246,17 @@
                 copy_of(kind, d, back).wait_recv()
                 start = PLACES[kind, d][0]
                 for item in items:
-                    at(item, d)[...] = received[pl.ds(start, item[4]), :]
+                    value = received[pl.ds(start, item[4]), :]
                     start += item[4]
+                    field, form, x, y, n = landed(item, d)
+                    if field in (RX, RY, RZ) and 0 <= x < 8 and 0 <= y < 8:
+                        mine = spot(field - RX + VX, form, x, y, n)
+                        mine[...] = mine[...] + spot(PUSH, form, x, y, n)[...] * value
+                    elif field in (RX, RY, RZ):
+                        rates = spot(field, form, x, y, n)
+                        rates[...] = rates[...] + value
+                    else:
+                        spot(field, form, x, y, n)[...] = value
 
     def outside(kind):
         for d, items in MESSAGES[kind].items():
@@ -254,8 +264,9 @@
             @pl.when(jnp.logical_not(there[-d[0], -d[1]]))
             def _():
                 for item in items:
-                    value = OPEN if item[0] == COH else 0.0
-                    at(item, d)[...] = jnp.full((item[4], 128), value, jnp.float32)
+                    if item[0] not in (RX, RY, RZ):
+                        value = OPEN if item[0] == COH else 0.0
+                        spot(*landed(item, d))[...] = jnp.full((item[4], 128), value, jnp.float32)
 
     depth = lax.broadcasted_iota(jnp.int32, (8, 128), 1)
 
@@ -290,18 +301,22 @@
     def backward_z(f):
         return NEAR * (f - deeper(f, -1)) + FAR * (deeper(f, 1) - deeper(f, -2))
 
+    nothing = jnp.zeros((8, 128), jnp.float32)
+    for field in (SXX, SXY, SXZ, SYY, SYZ):
+        for x in (-2, -1, 8, 9):
+            put(field, x, -4, "B", nothing)
+            put(field, x, 4, "B", nothing)
+        for y in (-2, -1, 8, 9):
+            put(field, 0, y, "F", nothing)
+    outside(0)
     loads[0].wait()
     for x in range(8):
         for field, c in ((SXX, 0), (SXY, 3), (SXZ, 4), (SYY, 1), (SYZ, 5)):
             put(field, x, 0, "B", stress[c, x])
-    pack(0)
-    pl.semaphore_wait(barrier, sum(there[d].astype(jnp.int32) for d in SIDES))
-    send(0)
-    for kind in range(3):
-        outside(kind)
-
-    for load in loads[1:]:
-        load.wait()
+
+    for k, load in enumerate(loads):
+        if k:
+            load.wait()
     place = cells[0]
     column = lax.broadcasted_iota(jnp.int32, (64, 128), 0) == (place // 128)
     spread = jnp.concatenate(
@@ -318,7 +333,7 @@
     for x in range(8):
         damping = jnp.where(absorb[x] == 1, SPONGE, 1.0)
         weight[0, x] = damping
-        weight[1, x] = H * material[2, x] * damping
+        put(PUSH, x, 0, "B", H * material[2, x] * damping)
         grown = 1.0 - 0.5 * anelastic[1, x]
         weight[2, x] = grown
         put(PP, x, 0, "B", H * grown * material[0, x])
@@ -336,18 +351,39 @@
     F_STARTS = (-1, 1)
 
     for step in range(STEPS):
-        kind = 3 * step
-        if step:
-            pack(kind)
-            send(kind)
+        kind = step
         for x in range(8):
             keep = 0.5 + 0.5 * anelastic[0, x]
             for c, field in enumerate(ALL):
                 base = stress[c, x] + source[pl.ds(c * 64 + x * 8, 8), :] - keep * memory[c, x]
                 put(field, x, 0, "B", base)
-        pack(kind + 1)
-        send(kind + 1)
-        receive(kind)
+        for field in (RX, RY, RZ):
+            for x in (-2, -1, 8, 9, 10):
+                put(field, x, -4, "B", nothing)
+                put(field, x, 4, "B", nothing)
+        for field, source_field, axis, reach in (
+            (RX, SXX, 0, -1),
+            (RY, SXY, 0, -2),
+            (RZ, SXZ, 0, -2),
+            (RY, SYY, 1, -1),
+            (RX, SXY, 1, -2),
+            (RZ, SYZ, 1, -2),
+        ):
+            factors = (-FAR, -NEAR, NEAR, FAR)
+            for i in (-2, -1, 8, 9, 10):
+                total = None
+                for k in range(4):
+                    j = i + reach + k
+                    if 0 <= j < 8:
+                        term = factors[k] * (
+                            view(source_field, j, 0, "B") if axis == 0 else view(source_field, 0, j, "F")
+                        )
+                        total = term if total is None else total + term
+                if axis == 0:
+                    if total is not None:
+                        put(field, i, 0, "B", total)
+                else:
+                    put(field, 0, i, "F", nothing if total is None else total)
         for x in range(8):
             rate_x = (
                 forward(SXX, x, 0, "B", 0) + backward(SXY, x, 0, "B", 1) + backward_z(stress[4, x])
@@ -358,16 +394,25 @@
             rate_z = (
                 backward(SXZ, x, 0, "B", 0) + backward(SYZ, x, 0, "B", 1) + forward_z(stress[2, x])
             )
-            damping, push = weight[0, x], weight[1, x]
+            damping, push = weight[0, x], view(PUSH, x, 0, "B")
             for c, (field, rate) in enumerate(((VX, rate_x), (VY, rate_y), (VZ, rate_z))):
-                new = velocity[c, x] * damping + push * rate
-                velocity[c, x] = new
-                put(field, x, 0, "B", new)
-        pack(kind + 2)
-        send(kind + 2)
+                before = view(field, x, 0, "B") if step else velocity[c, x]
+                put(field, x, 0, "B", before * damping + push * rate)
+        pack(kind)
+        if step == 0:
+            pl.semaphore_wait(barrier, sum(there[d].astype(jnp.int32) for d in SIDES))
+        send(kind)
         last = step == STEPS - 1
-        receive(kind + 1)
-        receive(kind + 2)
+        receive(kind)
+        for field, rates in ((VX, RX), (VY, RY), (VZ, RZ)):
+            beside = [(x, y, "B") for x in (-2, -1, 8, 9, 10) for y in (-4, 4)]
+            for x, y, form in beside + [(0, y, "F") for y in (-2, -1, 8, 9, 10)]:
+                new = view(field, x, y, form) + view(PUSH, x, y, form) * view(rates, x, y, form)
+                put(field, x, y, form, new)
+        if last:
+            for x in range(8):
+                for c, field in enumerate((VX, VY, VZ)):
+                    velocity[c, x] = view(field, x, 0, "B")
 
         def shear_xy(x, y, form):
             return forward(VX, x, y, form, 1) + forward(VY, x, y, form, 0)

time: 33.8 us -> 29.1 us (0.86)
  Pallas kernels: 32.9 us -> 28.1 us
    pallas_call x1, Pallas kernels: 32.1 us -> 27.3 us  [shards(): pl.pallas_call(functools.partial(kernel, n_gx, n_gy), out_shape=[pltpu.VM...]
where the time goes in v3:
time: 29.1 us; the launch traced here: 28.7 us
  Pallas kernels  28.1 us (97%)
  between operations  0.64 us (2%)
    pallas_call x1, Pallas kernels, shards(): pl.pallas_call(functools.partial(kernel, n_gx, n_gy), out_shape=[pltpu.VM...  27.3 us
    pallas_call x1, Pallas kernels, shards(): pl.pallas_call(hand_over, out_shape=[jax.ShapeDtypeStruct(r.shape, r.dtyp...  0.8 us

profile of v3, /device:TPU:1, one launch (start us, length us, event | category | flops | bytes accessed | tf_op | source)
XLA Modules:
  0.0 28.7 jit_solution(4151146011179711817)
XLA Ops:
  0.6 27.3 %waves.1 = (f32[3,8,8,128]{3,2,1,0:T(8,128)S(1)}, f32[6,8,8,128]{3,2,1,0:T(8,128)S(1)}, f32[6,8,8,128]{3,2,1,0:T(8,128)S(1)}) custom-call(f32[3,8,8,128]{3,2,1,0:T(8,128)} %velocity_in.1, f32[6,8,8,128]{3,2,1,0:T(8,128)} %stress_in.1, f32[6,8,8,128]{3,2,1,0:T(8,128)} %memory_in.1, f32[3,8,8,128]{3,2,1,0:T(8,128)} %material_in.1, ...), custom_call_target="tpu_custom_call" | custom-call | tf_op jit(solution)/shard_map/waves/pallas_call | solution.py:570
  27.9 0.8 %results.1 = (f32[3,8,8,128]{3,2,1,0:T(8,128)}, f32[6,8,8,128]{3,2,1,0:T(8,128)}, f32[6,8,8,128]{3,2,1,0:T(8,128)}) custom-call(f32[3,8,8,128]{3,2,1,0:T(8,128)S(1)} %get-tuple-element.6.refs_0_, f32[6,8,8,128]{3,2,1,0:T(8,128)S(1)} %get-tuple-element.7.refs_1_, f32[6,8,8,128]{3,2,1,0:T(8,128)S(1)} %get-tuple-element.8.refs_2_), custom_call_target="tpu_custom_call" | custom-call | tf_op jit(solution)/shard_map/results/pallas_call | solution.py:600

commit v4 on v3

--- a/solution.py
+++ b/solution.py
@@ -214,6 +214,7 @@
 
     def copy_of(kind, d, sem_side):
         start, n, k = PLACES[kind, d]
+        n = sum(item[4] for item in MESSAGES[kind][d])
         return pltpu.make_async_remote_copy(
             src_ref=sent.at[pl.ds(start, n)],
             dst_ref=received.at[pl.ds(start, n)],
@@ -231,7 +232,7 @@
                 start += item[4]
 
     def send(kind):
-        for d in MESSAGES[kind]:
+        for d in CORNERS + FACES:
 
             @pl.when(there[d])
             def _():

time: 29.1 us -> 28 us (0.962)
  Pallas kernels: 28.1 us -> 27.2 us
    pallas_call x1, Pallas kernels: 27.3 us -> 26.4 us  [shards(): pl.pallas_call(functools.partial(kernel, n_gx, n_gy), out_shape=[pltpu.VM...]
where the time goes in v4:
time: 28 us; the launch traced here: 27.8 us
  Pallas kernels  27.2 us (97%)
  between operations  0.64 us (2%)
    pallas_call x1, Pallas kernels, shards(): pl.pallas_call(functools.partial(kernel, n_gx, n_gy), out_shape=[pltpu.VM...  26.4 us
    pallas_call x1, Pallas kernels, shards(): pl.pallas_call(hand_over, out_shape=[jax.ShapeDtypeStruct(r.shape, r.dtyp...  0.8 us

profile of v4, /device:TPU:1, one launch (start us, length us, event | category | flops | bytes accessed | tf_op | source)
XLA Modules:
  0.0 27.8 jit_solution(1575676461950967679)
XLA Ops:
  0.6 26.4 %waves.1 = (f32[3,8,8,128]{3,2,1,0:T(8,128)S(1)}, f32[6,8,8,128]{3,2,1,0:T(8,128)S(1)}, f32[6,8,8,128]{3,2,1,0:T(8,128)S(1)}) custom-call(f32[3,8,8,128]{3,2,1,0:T(8,128)} %velocity_in.1, f32[6,8,8,128]{3,2,1,0:T(8,128)} %stress_in.1, f32[6,8,8,128]{3,2,1,0:T(8,128)} %memory_in.1, f32[3,8,8,128]{3,2,1,0:T(8,128)} %material_in.1, ...), custom_call_target="tpu_custom_call" | custom-call | tf_op jit(solution)/shard_map/waves/pallas_call | solution.py:571
  27.0 0.8 %results.1 = (f32[3,8,8,128]{3,2,1,0:T(8,128)}, f32[6,8,8,128]{3,2,1,0:T(8,128)}, f32[6,8,8,128]{3,2,1,0:T(8,128)}) custom-call(f32[3,8,8,128]{3,2,1,0:T(8,128)S(1)} %get-tuple-element.6.refs_0_, f32[6,8,8,128]{3,2,1,0:T(8,128)S(1)} %get-tuple-element.7.refs_1_, f32[6,8,8,128]{3,2,1,0:T(8,128)S(1)} %get-tuple-element.8.refs_2_), custom_call_target="tpu_custom_call" | custom-call | tf_op jit(solution)/shard_map/results/pallas_call | solution.py:601

commit v5 on v4

--- a/solution.py
+++ b/solution.py
@@ -115,7 +115,13 @@
     return -(-sum(item[4] for item in items) // 8) * 8
 
 
-MESSAGES = [{d: ONCE[d] + EACH_STEP[d] for d in SIDES}, EACH_STEP]
+def parts(table):
+    fields = (VX, VY, VZ, RX, RY, RZ, PUSH)
+    early = {d: [i for i in table[d] if i[0] in fields or d in CORNERS] for d in SIDES}
+    return early, {d: [i for i in table[d] if i[0] not in fields] for d in FACES}
+
+
+MESSAGES = [*parts({d: ONCE[d] + EACH_STEP[d] for d in SIDES}), *parts(EACH_STEP)]
 
 PLACES = {}
 used = 0
@@ -224,15 +230,16 @@
             device_id_type=MESH,
         )
 
-    def pack(kind):
-        for d, items in MESSAGES[kind].items():
+    def pack(kind, sides):
+        for d in sides:
+            items = MESSAGES[kind][d]
             start = PLACES[kind, d][0]
             for item in items:
                 sent[pl.ds(start, item[4]), :] = at(item)[...]
                 start += item[4]
 
-    def send(kind):
-        for d in CORNERS + FACES:
+    def send(kind, sides):
+        for d in sides:
 
             @pl.when(there[d])
             def _():
@@ -310,6 +317,7 @@
         for y in (-2, -1, 8, 9):
             put(field, 0, y, "F", nothing)
     outside(0)
+    outside(1)
     loads[0].wait()
     for x in range(8):
         for field, c in ((SXX, 0), (SXY, 3), (SXZ, 4), (SYY, 1), (SYZ, 5)):
@@ -352,7 +360,7 @@
     F_STARTS = (-1, 1)
 
     for step in range(STEPS):
-        kind = step
+        kind = 2 * step
         for x in range(8):
             keep = 0.5 + 0.5 * anelastic[0, x]
             for c, field in enumerate(ALL):
@@ -399,10 +407,17 @@
             for c, (field, rate) in enumerate(((VX, rate_x), (VY, rate_y), (VZ, rate_z))):
                 before = view(field, x, 0, "B") if step else velocity[c, x]
                 put(field, x, 0, "B", before * damping + push * rate)
-        pack(kind)
+        pack(kind, CORNERS)
         if step == 0:
+            pack(kind, FACES)
+            pack(kind + 1, FACES)
             pl.semaphore_wait(barrier, sum(there[d].astype(jnp.int32) for d in SIDES))
-        send(kind)
+        send(kind, CORNERS)
+        for part in (kind, kind + 1):
+            for d in FACES:
+                if step:
+                    pack(part, [d])
+                send(part, [d])
         last = step == STEPS - 1
         receive(kind)
         for field, rates in ((VX, RX), (VY, RY), (VZ, RZ)):
@@ -464,6 +479,7 @@
                 put_shear(field, x, 0, "B", trial[c])
                 centre[x, 3 + c] = trial[c]
             keep_centre(x, x, 0, "B", trial[:3])
+        receive(kind + 1)
         beyond = [(8, 8, 0, "B")] + [(9 + k, x, 8, "F") for k, x in enumerate(F_STARTS)]
         for k, x, y, form in beyond:
             parts = normal(x, y, form)

time: 28 us -> 27.8 us (level)
  no operation moved by 1% of the time
where the time goes in v5:
time: 27.8 us; the launch traced here: 27.6 us
  Pallas kernels  27 us (97%)
  between operations  0.64 us (2%)
    pallas_call x1, Pallas kernels, shards(): pl.pallas_call(functools.partial(kernel, n_gx, n_gy), out_shape=[pltpu.VM...  26.2 us
    pallas_call x1, Pallas kernels, shards(): pl.pallas_call(hand_over, out_shape=[jax.ShapeDtypeStruct(r.shape, r.dtyp...  0.8 us

profile of v5, /device:TPU:1, one launch (start us, length us, event | category | flops | bytes accessed | tf_op | source)
XLA Modules:
  0.0 27.6 jit_solution(3252082672135126002)
XLA Ops:
  0.6 26.2 %waves.1 = (f32[3,8,8,128]{3,2,1,0:T(8,128)S(1)}, f32[6,8,8,128]{3,2,1,0:T(8,128)S(1)}, f32[6,8,8,128]{3,2,1,0:T(8,128)S(1)}) custom-call(f32[3,8,8,128]{3,2,1,0:T(8,128)} %velocity_in.1, f32[6,8,8,128]{3,2,1,0:T(8,128)} %stress_in.1, f32[6,8,8,128]{3,2,1,0:T(8,128)} %memory_in.1, f32[3,8,8,128]{3,2,1,0:T(8,128)} %material_in.1, ...), custom_call_target="tpu_custom_call" | custom-call | tf_op jit(solution)/shard_map/waves/pallas_call | solution.py:587
  26.8 0.8 %results.1 = (f32[3,8,8,128]{3,2,1,0:T(8,128)}, f32[6,8,8,128]{3,2,1,0:T(8,128)}, f32[6,8,8,128]{3,2,1,0:T(8,128)}) custom-call(f32[3,8,8,128]{3,2,1,0:T(8,128)S(1)} %get-tuple-element.6.refs_0_, f32[6,8,8,128]{3,2,1,0:T(8,128)S(1)} %get-tuple-element.7.refs_1_, f32[6,8,8,128]{3,2,1,0:T(8,128)S(1)} %get-tuple-element.8.refs_2_), custom_call_target="tpu_custom_call" | custom-call | tf_op jit(solution)/shard_map/results/pallas_call | solution.py:617
